TPU v7x, 32 devices: a whole 2x2x4 slice. The times are simulated.
32 devices in a mesh: wide: 8 (over y, x, core), narrow: 4 (over z).
Axes of the slice: x: 2, y: 2, z: 4, core: 2. Of those that a mesh axis runs over, the one named last changes fastest.
Arguments:
- patches: bfloat16 [6400, 4, 512], P(('wide', 'narrow')), may hold values from -6 to 6
- window_extent: int32 [64, 2], P('wide'), may hold values from 1 to 10, as said below
- merge_gain: float32 [2048], replicated, may hold values from 0.5 to 1.5
- merge_shift: float32 [2048], replicated, may hold values from -2 to 2
- merge_weight: bfloat16 [2048, 1024], replicated, may hold values from -0.125 to 0.125
- norm1_gain: float32 [1024], replicated, may hold values from 0.5 to 1.5
- norm1_shift: float32 [1024], replicated, may hold values from -2 to 2
- qkv_weight: bfloat16 [1024, 3072], replicated, may hold values from -0.25 to 0.25
- qkv_bias: float32 [3072], replicated, may hold values from -2 to 2
- rel_table: float32 [361, 32], P(None, 'narrow'), may hold values from -4 to 4
- proj_weight: bfloat16 [1024, 1024], P('narrow'), may hold values from -0.5 to 0.5
- proj_bias: float32 [1024], replicated, may hold values from -2 to 2
- norm2_gain: float32 [1024], replicated, may hold values from 0.5 to 1.5
- norm2_shift: float32 [1024], replicated, may hold values from -2 to 2
- fc1_weight: bfloat16 [1024, 4096], P(None, 'narrow'), may hold values from -0.1875 to 0.1875
- fc1_bias: float32 [4096], P('narrow'), may hold values from -2 to 2
- fc2_weight: bfloat16 [4096, 1024], P('narrow'), may hold values from -0.125 to 0.125
- fc2_bias: float32 [1024], replicated, may hold values from -2 to 2
- out_grad: bfloat16 [6400, 1024], P('wide'), may hold values from -6 to 6
Outputs:
- output: bfloat16 [6400, 1024], P(('wide', 'narrow'))
- patches_grad: bfloat16 [6400, 4, 512], P(('wide', 'narrow'))
- merge_gain_grad: float32 [2048], replicated
- merge_shift_grad: float32 [2048], replicated
- merge_weight_grad: float32 [2048, 1024], P(('wide', 'narrow'))
- norm1_gain_grad: float32 [1024], replicated
- norm1_shift_grad: float32 [1024], replicated
- qkv_weight_grad: float32 [1024, 3072], P(('wide', 'narrow'))
- qkv_bias_grad: float32 [3072], replicated
- rel_table_grad: float32 [361, 32], replicated
- proj_weight_grad: float32 [1024, 1024], P(('narrow', 'wide'))
- proj_bias_grad: float32 [1024], replicated
- norm2_gain_grad: float32 [1024], replicated
- norm2_shift_grad: float32 [1024], replicated
- fc1_weight_grad: float32 [1024, 4096], P('wide', 'narrow')
- fc1_bias_grad: float32 [4096], P(('narrow', 'wide'))
- fc2_weight_grad: float32 [4096, 1024], P(('narrow', 'wide'))
- fc2_bias_grad: float32 [1024], replicated
Inputs may be any that keep to these rules, and one draw needn't show every extreme that they name: `window_extent`: each window's rows and columns on its page; many windows are whole, and window 0 is.
All inputs are finite; a program needn't handle non-finite values.
Results may differ from a plain program's by a relative error of at most 0.02.
Values may be sent and summed in bfloat16 or wider, within the bound.
No kernel may reach another device: no remote copies, remote signals or barrier semaphores. Data moves between devices by JAX's collectives and lax.ppermute only.
A program may use at most 128 MiB of HBM per device.

v0:
```python
import functools

import jax
import jax.numpy as jnp
from jax import lax
from jax.experimental import pallas as pl
from jax.experimental.pallas import tpu as pltpu
from jax.sharding import PartitionSpec as P

WIN = 10
WINDOW_TOKENS = WIN * WIN
QUERY_ROWS = 112
KEY_ROWS = 128
EPS = 1e-05
MEBI = 1024 * 1024
PROBS_ROOM = 52
WAIT_US = 100.0
WEIGHT_US = {"back1": 20, "proj_grad": 20, "back0": 20, "second_join": 20, "proj_join": 20}
WEIGHT_US |= dict.fromkeys(
    ("pack", "front", "cut", "pieces", "spread", "attend", "mine", "after", "slope", "feed", "second", "fc1_grad",
     "fc2_grad", "fc1_join", "fc2_join", "fc1_join2", "fc2_join2"), WAIT_US
)
FLOPS_PER_US = 10**9
BF = jnp.bfloat16
F32 = jnp.float32


def normalise(values):
    average = jnp.mean(values, -1, keepdims=True)
    centred = values - average
    inverse = lax.rsqrt(jnp.mean(centred * centred, -1, keepdims=True) + EPS)
    return centred * inverse, inverse


def norm_backward(grad_out, normal, inverse, gain):
    scaled = grad_out * gain
    return inverse * (
        scaled
        - jnp.mean(scaled, -1, keepdims=True)
        - normal * jnp.mean(scaled * normal, -1, keepdims=True)
    )


def matmul(left, right):
    return jnp.dot(left, right, preferred_element_type=jnp.float32)


def contract(left, right, left_dim, right_dim):
    return lax.dot_general(
        left, right, (((left_dim,), (right_dim,)), ((), ())), preferred_element_type=jnp.float32
    )


def low(array):
    return array.astype(BF)


def row(vector):
    return vector.reshape(1, -1)


def stays():
    return pl.BlockSpec(memory_space=pl.ANY)


def outside():
    return pl.BlockSpec(memory_space=pltpu.HBM)


def held():
    return pl.BlockSpec(memory_space=pltpu.VMEM)


def shape_of(shape, dtype):
    return jax.ShapeDtypeStruct(shape, dtype)


def whole(
    kernel, place, outs, *operands, leave=(), scratch=(), after=(), through=(), room=20, name=None
):
    arrays = [a for a, _ in operands]
    count, skip, given = len(arrays), len(after) + len(through), len(outs)

    def body(place_ref, *refs):
        own_outs = refs[count + skip : count + skip + given]
        kernel(place_ref, *refs[:count], *own_outs, *refs[count + skip + given + len(through) :])

    return pl.pallas_call(
        body,
        in_specs=[pl.BlockSpec(memory_space=pltpu.SMEM)]
        + [{True: held, False: outside, None: stays}[inside]() for _, inside in operands]
        + [stays()] * skip,
        out_specs=[outside() if k in leave else held() for k in range(given)]
        + [stays()] * len(through),
        out_shape=list(outs) + [shape_of(a.shape, a.dtype) for a in through],
        input_output_aliases={1 + count + len(after) + k: given + k for k in range(len(through))},
        scratch_shapes=list(scratch),
        compiler_params=pltpu.CompilerParams(vmem_limit_bytes=room * MEBI),
        cost_estimate=pl.CostEstimate(
            flops=int(WEIGHT_US.get(name, 5) * FLOPS_PER_US), bytes_accessed=0, transcendentals=0
        ),
        name=name,
    )(place, *arrays, *after, *through)


def tie(array, *after):
    def body(*refs):
        del refs

    return pl.pallas_call(
        body,
        in_specs=[stays()] * (1 + len(after)),
        out_specs=stays(),
        out_shape=shape_of(array.shape, array.dtype),
        input_output_aliases={0: 0},
        name="tie",
    )(array, *after)


def swap(array, axis, mask):
    size = lax.axis_size(axis)
    return lax.ppermute(array, axis, [(i, i ^ mask) for i in range(size)])


def turn(array, axis, step):
    size = lax.axis_size(axis)
    return lax.ppermute(array, axis, [(i, (i + step) % size) for i in range(size)])


def sum_all(vector):
    mask = 1
    while mask < lax.axis_size("wide"):
        vector = vector + swap(vector, "wide", mask)
        mask *= 2
    mask = 1
    while mask < lax.axis_size("narrow"):
        vector = vector + swap(vector, "narrow", mask)
        mask *= 2
    return vector


def sum_high(parts, high):
    take = lambda index: lax.dynamic_index_in_dim(parts, index, 0, keepdims=False)
    total = take(high).astype(F32)
    for j in range(1, parts.shape[0]):
        total = total + swap(low(take(high ^ j)), "wide", 8 * j).astype(F32)
    return total


def grad_kernel(place_ref, *refs, lefts, rights, block, rows, riding):
    left_refs, right_refs = refs[: len(lefts)], refs[len(lefts) : len(lefts) + len(rights)]
    kept_ref, sent_ref, total_ref = refs[-3:]
    core = place_ref[1]
    if riding:
        give_sums(sent_ref, kept_ref.shape[0], refs[-4][...])

    @pl.loop(0, kept_ref.shape[0])
    def _(step):
        at = pl.ds(pl.multiple_of(step * block, block), block)
        total = None
        for l_ref, l_at, r_ref, r_at in zip(left_refs, lefts, right_refs, rights):
            left = l_ref[:, at] if l_at is None else l_ref[l_at, :, at]
            right = r_ref[: left.shape[0]] if r_at is None else r_ref[r_at]
            right = low(right)
            part = contract(left, right, 0, 0)
            total = part if total is None else total + part
        total_ref[...] = total
        for s in range(block // (2 * rows)):
            mine = pl.multiple_of((2 * s + core) * rows, rows)
            theirs = pl.multiple_of((2 * s + 1 - core) * rows, rows)
            kept_ref[step, s * rows : (s + 1) * rows] = total_ref[pl.ds(mine, rows)]
            sent_ref[step, s * rows : (s + 1) * rows] = low(total_ref[pl.ds(theirs, rows)])


def grad_call(place, lefts, rights, block, rows, name, after=(), sums=None):
    split = lambda item: item if isinstance(item, tuple) else (item, None)
    left_arrays, left_at = zip(*map(split, lefts))
    right_arrays, right_at = zip(*map(split, rights))
    deep, width = left_arrays[0].shape[-1], right_arrays[0].shape[-1]
    shape = (deep // block, block // 2, width)
    return whole(
        functools.partial(
            grad_kernel, lefts=left_at, rights=right_at, block=block, rows=rows,
            riding=sums is not None,
        ),
        place,
        [shape_of(shape, F32), shape_of((shape[0] + (sums is not None), *shape[1:]), BF)],
        *((a, True) for a in left_arrays + right_arrays + (() if sums is None else (sums,))),
        scratch=[pltpu.VMEM((block, width), F32)],
        after=after,
        name=name,
    )


def add_up(refs, lead, rows):
    total = None
    for ref in refs:
        part = ref[lead, rows, :].astype(F32)
        total = part if total is None else total + part
    return total


def join_call(place, groups, outs, name, after=(), through=(), sums=None):
    width = groups[0][0].shape[2]
    counts = [len(sources) for sources in groups]
    count = sum(counts)
    rows_of = [pieces[0]((0, 0, 0))[3] for _, pieces in outs]
    more = -(-sums[0].shape[0] // rows_of[1]) if sums else 0
    shapes = [
        shape_of((len(pieces) + (more if k else 0), rows, width), dtype)
        for k, ((dtype, pieces), rows) in enumerate(zip(outs, rows_of))
    ]
    if sums:
        shapes = [shape_of(sums[0].shape, F32)] + shapes

    def kernel(place_ref, *refs):
        place_now = (place_ref[0], place_ref[1], place_ref[2])
        ins, out_refs = refs[:count], refs[count:]
        if sums:
            own_ref, total_ref, out_refs = refs[count], refs[count + 1], refs[count + 2 :]
            total = own_ref[...] + take_sums(ins[counts[0] - 1], sums[1], own_ref.shape[0])
            total_ref[...] = total
        at = [sum(counts[:g]) for g in range(len(counts))]
        for k, (out_ref, (dtype, pieces)) in enumerate(zip(out_refs, outs)):
            for n, piece in enumerate(pieces):
                group, lead, start, rows = piece(place_now)
                if not isinstance(start, int):
                    start = pl.multiple_of(start, rows)
                part = add_up(ins[at[group] : at[group] + counts[group]], lead, pl.ds(start, rows))
                out_ref[n] = part.astype(dtype)
            if sums and k:
                give_sums(out_ref, len(pieces), total)

    arrays = [s for sources in groups for s in sources] + ([sums[0]] if sums else [])
    return whole(
        kernel, place, shapes, *((s, True) for s in arrays), after=after, through=through, name=name
    )


def give_sums(ref, first, values):
    parts = low(values)
    size = ref.shape[1]
    for k in range(parts.shape[0] // size):
        ref[first + k] = parts[k * size : (k + 1) * size]
    rest = parts.shape[0] % size
    if rest:
        ref[first + parts.shape[0] // size, :rest] = parts[parts.shape[0] - rest :]


def take_sums(ref, first, rows):
    size = ref.shape[1]
    blocks = [ref[first + k].astype(F32) for k in range(-(-rows // size))]
    return (jnp.concatenate(blocks, 0) if len(blocks) > 1 else blocks[0])[:rows]


def cut_kernel(place_ref, merged_ref, own_ref, sent_ref, onward_ref):
    quad = place_ref[2]
    lanes = own_ref.shape[1]
    take = lambda j: merged_ref[:, pl.ds(pl.multiple_of((quad ^ j) * lanes, lanes), lanes)]
    own_ref[...] = take(0)
    sent_ref[0] = take(2)
    sent_ref[1] = take(3)
    onward_ref[...] = take(1)


def pack_kernel(
    place_ref, proj_ref, table_ref, message_ref
):
    part = proj_ref.shape[0] // 8
    own_heads = table_ref.shape[1]
    room = message_ref.shape[1] // 2
    eighth = place_ref[2] * 2 + place_ref[1]
    message_ref[:part] = proj_ref[pl.ds(pl.multiple_of(eighth * part, part), part), :]
    offsets = table_ref.shape[0]
    table = jnp.concatenate(
        [table_ref[...], jnp.zeros((offsets, 128 - own_heads), F32)], 1
    )
    table = jnp.concatenate([table, jnp.zeros((room - offsets, 128), F32)], 0)
    table = jnp.transpose(table)[:own_heads]
    high = low(table).astype(F32)
    rows = jnp.concatenate([high, table - high], 1)
    spare = message_ref.shape[0] - part - own_heads
    message_ref[part:] = low(jnp.concatenate([rows, jnp.zeros((spare, 2 * room), F32)], 0))


def pieces_kernel(place_ref, *refs, part):
    del place_ref
    for j, ref in enumerate(refs[:-1]):
        refs[-1][j * part : (j + 1) * part] = ref[:part]


def front_kernel(
    place_ref, flat_ref, mg_ref, ms_ref, n1g_ref, n1s_ref, qb_ref, mw_any, qw_any,
    merged_ref, resid0_ref, normed1_ref, qkv_ref, mw_ref, qw_ref, sems,
):
    copy_m = pltpu.make_async_copy(mw_any, mw_ref, sems.at[0])
    copy_q = pltpu.make_async_copy(qw_any, qw_ref, sems.at[1])
    copy_m.start()
    copy_q.start()
    hat, _ = normalise(flat_ref[...].astype(F32))
    merged = low(hat * mg_ref[...] + ms_ref[...])
    merged_ref[...] = merged
    copy_m.wait()
    resid0 = matmul(merged, mw_ref[...])
    resid0_ref[...] = resid0
    hat1, _ = normalise(resid0)
    normed1 = low(hat1 * n1g_ref[...] + n1s_ref[...])
    normed1_ref[...] = normed1
    copy_q.wait()
    qkv_ref[...] = low(matmul(normed1, qw_ref[...]) + qb_ref[...])


def front_call(place, flat, mg, ms, n1g, n1s, qb, mw, qw):
    rows, deep = flat.shape
    width = mw.shape[1]
    return whole(
        front_kernel,
        place,
        [
            shape_of((rows, deep), BF),
            shape_of((rows, width), F32),
            shape_of((rows, width), BF),
            shape_of((rows, 3 * width), BF),
        ],
        (flat, True), (row(mg), True), (row(ms), True), (row(n1g), True), (row(n1s), True),
        (row(qb), True), (mw, False), (qw, False),
        scratch=[
            pltpu.VMEM(mw.shape, BF), pltpu.VMEM(qw.shape, BF), pltpu.SemaphoreType.DMA((2,)),
        ],
        room=28,
        name="front",
    )


def mine_kernel(place_ref, *refs):
    del place_ref
    rows = refs[0].shape[0]
    for q, ref in enumerate(refs[:-1]):
        refs[-1][q * rows : (q + 1) * rows] = ref[...]


def whole_proj(place_ref, own_ref, mine_ref, theirs_ref, proj_ref, groups):
    rank, core, quad = place_ref[0], place_ref[1], place_ref[2]
    shard = own_ref.shape[0]
    part = shard // 8
    proj_ref[pl.ds(pl.multiple_of(rank * shard, shard), shard), :] = own_ref[...]
    for k in range(4 * (groups - 1)):
        q, j = k // (groups - 1), k % (groups - 1)
        base = lax.rem(rank + groups - 1 - j, groups) * shard + (quad ^ q) * 2 * part
        rows = slice(k * part, (k + 1) * part)
        proj_ref[pl.ds(pl.multiple_of(base + core * part, part), part), :] = mine_ref[rows]
        proj_ref[pl.ds(pl.multiple_of(base + (1 - core) * part, part), part), :] = theirs_ref[rows]


def after_kernel(
    place_ref, heads_ref, resid0_ref, pb_ref, n2g_ref, n2s_ref, own_ref, mine_ref, theirs_ref,
    resid1_ref, normed2_ref, proj_ref, *, groups,
):
    whole_proj(place_ref, own_ref, mine_ref, theirs_ref, proj_ref, groups)
    resid1 = resid0_ref[...] + matmul(heads_ref[...], proj_ref[...]) + pb_ref[...]
    resid1_ref[...] = resid1
    hat2, _ = normalise(resid1)
    normed2_ref[...] = low(hat2 * n2g_ref[...] + n2s_ref[...])


SQRT_HALF = 0.5**0.5
DENSITY = 0.3989422804014327


def gelu_pair(values):
    below = 0.5 * (1.0 + lax.erf(values * SQRT_HALF))
    density = jnp.exp(-0.5 * values * values) * DENSITY
    return values * below, below + values * density


def slope_kernel(
    place_ref, dy_ref, fc2_ref, rows_ref, own_ref, out_ref, wide_ref, *, groups, pad, chunk
):
    tokens, width = own_ref.shape
    wide_ref[...] = dy_ref[...].astype(F32)
    fill = jnp.zeros((pad - tokens, width), F32)
    for j in range(groups):
        at = lax.rem(place_ref[0] + groups - j, groups) * tokens
        block = wide_ref[pl.ds(pl.multiple_of(at, 8), tokens), :]
        rows_ref[j * pad : (j + 1) * pad] = low(jnp.concatenate([block, fill], 0))
        if j == 0:
            own_ref[...] = low(block)

    @pl.loop(0, fc2_ref.shape[0] // chunk)
    def _(step):
        at = pl.ds(pl.multiple_of(step * chunk, chunk), chunk)
        out_ref[:, at] = contract(rows_ref[...], fc2_ref[at, :], 1, 1)


def feed_kernel(
    place_ref, n0_ref, n1_ref, n2_ref, n3_ref, d_act_ref, fc1_ref, fc1b_ref,
    act_ref, dpre_ref, all_ref, db_ref, o0_ref, o1_ref, o2_ref, o3_ref, *, pad, chunk,
):
    del place_ref
    rows, width = n0_ref.shape
    for j, ref in enumerate((n0_ref, n1_ref, n2_ref, n3_ref)):
        all_ref[j * pad : j * pad + rows, :] = ref[...]
        all_ref[j * pad + rows : (j + 1) * pad, :] = jnp.zeros((pad - rows, width), BF)

    @pl.loop(0, fc1_ref.shape[1] // chunk)
    def _(step):
        at = pl.ds(pl.multiple_of(step * chunk, chunk), chunk)
        pre = matmul(all_ref[...], fc1_ref[:, at]) + fc1b_ref[:, at]
        act, slope = gelu_pair(pre)
        act_ref[:, at] = low(act)
        d_low = low(d_act_ref[:, at] * slope)
        dpre_ref[:, at] = d_low
        db_ref[:, at] = jnp.sum(d_low.astype(F32), 0, keepdims=True)

    for j, ref in enumerate((o0_ref, o1_ref, o2_ref, o3_ref)):
        part = contract(dpre_ref[j * pad : (j + 1) * pad, :], fc1_ref[...], 1, 1)
        ref[...] = low(part[:rows])


def second_kernel(place_ref, act_ref, fc2_ref, kept_ref, sent_ref, *, pad, groups):
    rank = place_ref[0]
    rows = kept_ref.shape[1]
    for ref, k, flip in ((sent_ref, 0, 1), (sent_ref, 1, 3), (kept_ref, 0, 0), (kept_ref, 1, 2)):
        block = lax.rem(rank + groups - (rank ^ flip), groups)
        at = pl.ds(pl.multiple_of(block * pad, pad), pad)
        ref[k] = low(matmul(act_ref[at, :], fc2_ref[...])[:rows])


def back2_kernel(
    place_ref, c0_ref, c1_ref, c2_ref, c3_ref, resid1_ref, dy_ref, n2g_ref, own_ref, mine_ref, theirs_ref,
    dresid1_ref, dheads_ref, proj_ref, *, groups,
):
    whole_proj(place_ref, own_ref, mine_ref, theirs_ref, proj_ref, groups)
    rows = dheads_ref.shape[0]
    d_norm2 = (
        c0_ref[...].astype(F32) + c1_ref[...].astype(F32)
        + c2_ref[...].astype(F32) + c3_ref[...].astype(F32)
    )
    hat2, inv2 = normalise(resid1_ref[...])
    dy = dy_ref[...].astype(F32)
    d_resid1 = dy + norm_backward(d_norm2, hat2, inv2, n2g_ref[...])
    dresid1_ref[:rows] = d_resid1
    sums = (d_resid1, d_norm2 * hat2, d_norm2, dy)
    for k, part in enumerate(sums):
        dresid1_ref[rows + k : rows + k + 1] = jnp.sum(part, 0, keepdims=True)
    dheads_ref[...] = low(contract(low(d_resid1), proj_ref[...], 1, 1))


def back1_kernel(
    place_ref, d0_ref, d1_ref, d2_ref, d3_ref, dresid1_ref, resid0_ref, n1g_ref, qw_any,
    dresid0_ref, sums_ref, qw_ref, sems,
):
    rows, width = resid0_ref.shape
    quad = place_ref[2]
    lanes = width // 4
    copies = [
        pltpu.make_async_copy(qw_any.at[:, pl.ds(i * width, width)], qw_ref.at[i], sems.at[i])
        for i in range(3)
    ]
    for copy in copies:
        copy.start()
    hat1, inv1 = normalise(resid0_ref[...])
    d_norm1 = jnp.zeros((rows, width), F32)
    for i in range(3):
        copies[i].wait()
        for j, d_ref in enumerate((d0_ref, d1_ref, d2_ref, d3_ref)):
            part = d_ref[:, i * lanes : (i + 1) * lanes]
            at = pl.ds(pl.multiple_of((quad ^ j) * lanes, lanes), lanes)
            d_norm1 = d_norm1 + contract(part, qw_ref[i, :, at], 1, 1)
            sums_ref[2 + i : 3 + i, at] = jnp.sum(part.astype(F32), 0, keepdims=True)
    dresid0_ref[...] = low(
        dresid1_ref[:rows] + norm_backward(d_norm1, hat1, inv1, n1g_ref[...])
    )
    sums_ref[0:1] = jnp.sum(d_norm1 * hat1, 0, keepdims=True)
    sums_ref[1:2] = jnp.sum(d_norm1, 0, keepdims=True)


def back0_kernel(
    place_ref, dresid0_ref, flat_ref, mg_ref, mw_any, grad_ref, sums_ref, mw_ref, sems
):
    del place_ref
    copy = pltpu.make_async_copy(mw_any, mw_ref, sems.at[0])
    copy.start()
    hat, inv = normalise(flat_ref[...].astype(F32))
    copy.wait()
    d_merged = contract(dresid0_ref[...], mw_ref[...], 1, 1)
    grad_ref[...] = low(norm_backward(d_merged, hat, inv, mg_ref[...]))
    width = dresid0_ref.shape[1]
    gain = jnp.sum(d_merged * hat, 0, keepdims=True)
    shift = jnp.sum(d_merged, 0, keepdims=True)
    for i in range(gain.shape[1] // width):
        sums_ref[i : i + 1] = gain[:, i * width : (i + 1) * width]
        sums_ref[2 + i : 3 + i] = shift[:, i * width : (i + 1) * width]


SPAN = 2 * WIN - 1
OFFSETS = 384
STRIP = 256


def strip_picks(column, offsets_first):
    shape, o_dim = ((OFFSETS, STRIP), 0) if offsets_first else ((STRIP, OFFSETS), 1)
    offset = lax.broadcasted_iota(jnp.int32, shape, o_dim)
    lane = lax.broadcasted_iota(jnp.int32, shape, 1 - o_dim)
    wanted = (SPAN - 1 - lane // WIN) * SPAN + column - lane % WIN + WIN - 1
    hit = (offset == wanted) & (lane < SPAN * WIN)
    return jnp.where(hit, 1.0, 0.0).astype(BF)


def split3(values):
    first = low(values)
    rest = values - first.astype(F32)
    second = low(rest)
    third = low(rest - second.astype(F32))
    return first, second, third


def spread_kernel(place_ref, m0_ref, m1_ref, m2_ref, m3_ref, bias_ref, table_ref, *, part, groups):
    heads = table_ref.shape[0]
    own_heads = heads // groups
    room = m0_ref.shape[1] // 2
    for j, ref in enumerate((m0_ref, m1_ref, m2_ref, m3_ref)):
        both = ref[part : part + 2 * own_heads, :].astype(F32)[:own_heads]
        at = pl.multiple_of(lax.rem(place_ref[0] + groups - j, groups) * own_heads, own_heads)
        table_ref[pl.ds(at, own_heads), :] = both[:, :OFFSETS] + both[:, room : room + OFFSETS]
    table = table_ref[...]
    high = low(table)
    table = jnp.concatenate([high, low(table - high.astype(F32))], 0)
    for column in range(WIN):
        parts = matmul(table, strip_picks(column, True))
        strip = parts[:heads] + parts[heads:]
        for r in range(WIN):
            start = (WIN - 1 - r) * WIN
            at = (r * WIN + column) * heads
            bias_ref[at : at + heads, :] = strip[:, start : start + KEY_ROWS]
    bias_ref[WINDOW_TOKENS * heads :, :] = jnp.zeros(
        ((QUERY_ROWS - WINDOW_TOKENS) * heads, KEY_ROWS), F32
    )


def fold(grad_ref, heads):
    total = jnp.zeros((3 * heads, OFFSETS), F32)
    for column in range(WIN):
        strip = jnp.zeros((heads, STRIP), F32)
        for r in range(WIN):
            start = (WIN - 1 - r) * WIN
            at = (r * WIN + column) * heads
            part = grad_ref[at : at + heads, :]
            wide = jnp.concatenate([part, jnp.zeros((heads, STRIP - KEY_ROWS), F32)], 1)
            strip = strip + (pltpu.roll(wide, start, 1) if start else wide)
        total = total + matmul(jnp.concatenate(split3(strip), 0), strip_picks(column, False))
    return total[:heads] + total[heads : 2 * heads] + total[2 * heads :]


def window_rows(values, window, rows):
    part = values.astype(F32)[window * WINDOW_TOKENS : (window + 1) * WINDOW_TOKENS]
    zeros = jnp.zeros((rows - WINDOW_TOKENS, part.shape[1]), F32)
    return low(jnp.concatenate([part, zeros], 0))


def stack_heads(part, heads, head_dim):
    lane = lax.broadcasted_iota(jnp.int32, part.shape, 1) // head_dim
    zero = jnp.zeros_like(part)
    return jnp.concatenate([jnp.where(lane == h, part, zero) for h in range(heads)], 0)


def attend_kernel(
    place_ref, qkv_ref, bias_ref, mask_ref, out_ref, probs_any, probs_ref, sems, *, windows, head_dim
):
    del place_ref
    width = out_ref.shape[1]
    lanes = width // 4

    def keep(step):
        return pltpu.make_async_copy(probs_ref.at[step], probs_any.at[step], sems.at[step])

    @pl.loop(0, 4)
    def _(step):
        attend_group(
            step, qkv_ref, bias_ref, mask_ref, out_ref, probs_ref, windows, head_dim, width, lanes
        )
        keep(step).start()

    for step in range(4):
        keep(step).wait()


def attend_group(
    step, qkv_ref, bias_ref, mask_ref, out_ref, probs_ref, windows, head_dim, width, lanes
):
    heads, all_heads = lanes // head_dim, width // head_dim
    first = step * heads
    scale = head_dim ** (-0.5)
    at = lambda kind: pl.ds(pl.multiple_of(kind * width + step * lanes, lanes), lanes)
    q_all, k_all, v_all = (qkv_ref[:, at(kind)] for kind in range(3))
    outs = []
    for w in range(windows):
        query = window_rows(q_all, w, QUERY_ROWS)
        keys = stack_heads(window_rows(k_all, w, KEY_ROWS), heads, head_dim)
        values = stack_heads(window_rows(v_all, w, KEY_ROWS), heads, head_dim)
        scores = contract(query, keys, 1, 1) * scale
        mask = mask_ref[w]
        rounded = []
        for h in range(heads):
            bias = bias_ref[pl.ds(first + h, QUERY_ROWS, stride=all_heads), :]
            raw = scores[:, h * KEY_ROWS : (h + 1) * KEY_ROWS] + bias + mask
            expo = jnp.exp(raw - jnp.max(raw, -1, keepdims=True))
            probs = expo / jnp.sum(expo, -1, keepdims=True)
            probs_ref[step, w, h] = probs
            rounded.append(low(probs))
        mixed = matmul(jnp.concatenate(rounded, 1), values)
        outs.append(mixed[:WINDOW_TOKENS])
    out_ref[:, at(0)] = low(jnp.concatenate(outs, 0))


def attend_back_kernel(
    place_ref, qkv_ref, grad_ref, probs_any, d0_ref, d1_ref, d2_ref, d3_ref, table_ref, dbias_ref, probs_ref, sems,
    *, windows, head_dim
):
    width = grad_ref.shape[1]

    def fetch(step):
        return pltpu.make_async_copy(
            probs_any.at[place_ref[2] ^ step], probs_ref.at[step], sems.at[step]
        )

    for step in range(4):
        fetch(step).start()

    @pl.loop(0, 4)
    def _(step):
        fetch(step).wait()
        attend_back_group(
            place_ref[2] ^ step, step, qkv_ref, grad_ref, probs_ref, (d0_ref, d1_ref, d2_ref, d3_ref), dbias_ref,
            windows, head_dim, width, width // 4,
        )

    table_ref[...] = fold(dbias_ref, table_ref.shape[0])


def attend_back_group(
    group, step, qkv_ref, grad_ref, probs_ref, d_refs, dbias_ref,
    windows, head_dim, width, lanes,
):
    heads, all_heads = lanes // head_dim, width // head_dim
    first = group * heads
    scale = head_dim ** (-0.5)
    at = lambda kind: pl.ds(pl.multiple_of(kind * width + group * lanes, lanes), lanes)
    q_all, k_all, v_all = (qkv_ref[:, at(kind)] for kind in range(3))
    g_all = grad_ref[:, at(0)]
    all_q, all_k, all_v = [], [], []
    d_first = []
    for w in range(windows):
        query = stack_heads(window_rows(q_all, w, QUERY_ROWS), heads, head_dim)
        keys = stack_heads(window_rows(k_all, w, KEY_ROWS), heads, head_dim)
        values = stack_heads(window_rows(v_all, w, KEY_ROWS), heads, head_dim)
        plain = window_rows(g_all, w, QUERY_ROWS)
        grad = stack_heads(plain, heads, head_dim)
        d_probs = contract(plain, values, 1, 1)
        d_list, p_list = [], []
        for h in range(heads):
            probs = probs_ref[step, w, h]
            part = d_probs[:, h * KEY_ROWS : (h + 1) * KEY_ROWS]
            total = jnp.sum(part * probs, -1, keepdims=True)
            d_scores = low(probs * (part - total))
            d_list.append(d_scores)
            p_list.append(low(probs))
            if w == 0:
                d_first.append(d_scores.astype(F32))
            else:
                d_first[h] = d_first[h] + d_scores.astype(F32)
            if w == windows - 1:
                dbias_ref[pl.ds(first + h, QUERY_ROWS, stride=all_heads), :] = d_first[h]
        d_query = matmul(jnp.concatenate(d_list, 1), keys) * scale
        d_keys = contract(jnp.concatenate(d_list, 0), query, 0, 0) * scale
        d_values = contract(jnp.concatenate(p_list, 0), grad, 0, 0)
        all_q.append(d_query[:WINDOW_TOKENS])
        all_k.append(d_keys[:WINDOW_TOKENS])
        all_v.append(d_values[:WINDOW_TOKENS])
    result = jnp.concatenate(
        [low(jnp.concatenate(parts, 0)) for parts in (all_q, all_k, all_v)], 1
    )

    for k, d_ref in enumerate(d_refs):

        @pl.when(step == k)
        def _(d_ref=d_ref):
            d_ref[...] = result


def spots(heads, lines, vectors):
    columns = 3
    return [(k // columns, OFFSETS + 128 * (k % columns)) for k in range(vectors * lines)]


def collect_kernel(place_ref, s0_ref, s1_ref, d_ref, rel_ref, b_ref, out_ref):
    heads = rel_ref.shape[0]
    lines = s0_ref.shape[1] // 128
    out_ref[...] = jnp.zeros(out_ref.shape, F32)
    out_ref[:heads, :OFFSETS] = rel_ref[...]
    vectors = [ref[r : r + 1, :] for ref in (s0_ref, s1_ref) for r in range(ref.shape[0])]
    after = d_ref.shape[0] - 8
    vectors += [d_ref[after + r : after + r + 1, :] for r in range(4)]
    for k, (at, lane) in enumerate(spots(heads, lines, len(vectors))):
        piece = vectors[k // lines][:, 128 * (k % lines) : 128 * (k % lines + 1)]
        out_ref[at : at + 1, lane : lane + 128] = piece
    own = b_ref.shape[1] // 128
    first = heads + pl.multiple_of((place_ref[0] // 2) * own, own)
    block = jnp.concatenate([b_ref[:, k * 128 : (k + 1) * 128] for k in range(own)], 0)
    side = place_ref[0] % 2

    @pl.when(side == 0)
    def _():
        out_ref[pl.ds(first, own), 0:128] = block

    @pl.when(side == 1)
    def _():
        out_ref[pl.ds(first, own), 128:256] = block


def deliver_kernel(place_ref, all_ref, *refs, heads):
    *vector_refs, rel_ref, b_ref = refs
    rel_ref[...] = all_ref[:heads, : rel_ref.shape[1]]
    lines = [ref.shape[0] // 128 for ref in vector_refs]
    places = iter(spots(heads, 1, sum(lines)))
    for ref, count in zip(vector_refs, lines):
        for k in range(count):
            at, lane = next(places)
            ref[128 * k : 128 * (k + 1)] = all_ref[at, lane : lane + 128]
    own = b_ref.shape[0]
    first = heads + pl.multiple_of((place_ref[0] // 2) * own, own)
    side = place_ref[0] % 2

    @pl.when(side == 0)
    def _():
        b_ref[...] = all_ref[pl.ds(first, own), 0:128]

    @pl.when(side == 1)
    def _():
        b_ref[...] = all_ref[pl.ds(first, own), 128:256]


def columns_kernel(place_ref, b0_ref, b1_ref, b2_ref, b3_ref, own_ref, out_ref, sums_ref):
    rows = out_ref.shape[0]
    lanes = b0_ref.shape[2] // 3
    total = own_ref[...]
    for j, ref in enumerate((b0_ref, b1_ref, b2_ref, b3_ref)):
        for part in range(3):
            at = pl.multiple_of((part * 4 + (place_ref[2] ^ j)) * lanes, lanes)
            out_ref[:, pl.ds(at, lanes)] = ref[0, :rows, part * lanes : (part + 1) * lanes].astype(F32)
        if j:
            total = total + take_sums(ref, 1, own_ref.shape[0])
    sums_ref[...] = total


def on_device(
    patches,
    window_extent,
    merge_gain,
    merge_shift,
    merge_weight,
    norm1_gain,
    norm1_shift,
    qkv_weight,
    qkv_bias,
    rel_table,
    proj_weight,
    proj_bias,
    norm2_gain,
    norm2_shift,
    fc1_weight,
    fc1_bias,
    fc2_weight,
    fc2_bias,
    out_grad,
):
    groups, wide = lax.axis_size("narrow"), lax.axis_size("wide")
    devices = wide * groups
    highs = wide // 8
    wide_at, rank = lax.axis_index("wide"), lax.axis_index("narrow")
    core, quad, high = wide_at % 2, (wide_at // 2) % 4, wide_at // 8
    place = jnp.stack([rank, core, quad]).astype(jnp.int32)
    tokens = patches.shape[0]
    width = qkv_weight.shape[0]
    own_heads = rel_table.shape[1]
    heads = own_heads * groups
    head_dim = width // heads
    windows = tokens // WINDOW_TOKENS
    pad = tokens + (-tokens) % 16

    def arrange(array, order):
        if highs == 1:
            return array
        sizes = {"h": highs, "q": 4, "c": 2, "n": groups}
        cut = [sizes[k] for k in order]
        rest = array.shape[1]
        for size in cut:
            rest //= size
        at = order.index("h") + 1
        moved = [i + 1 for i in range(len(order)) if i + 1 != at] + [at, len(order) + 1]
        return jnp.transpose(array.reshape(-1, *cut, rest), [0] + moved).reshape(array.shape)

    def settle(array):
        if highs == 1:
            return array[0]
        return sum_high(array[0].reshape(highs, -1, array.shape[2]), high)

    part = proj_weight.shape[0] // 8
    message = whole(
        pack_kernel,
        place,
        [shape_of((part + own_heads + (-(part + own_heads)) % 16, width), BF)],
        (proj_weight, True),
        (rel_table, True),
        name="pack",
    )[0]
    messages = [turn(message, "narrow", step) for step in range(1, groups)]

    flat = patches.reshape(tokens, -1)
    merged, resid0, normed1, qkv = front_call(
        place, flat, merge_gain, merge_shift, norm1_gain, norm1_shift, qkv_bias,
        merge_weight, qkv_weight,
    )
    mine = whole(
        functools.partial(pieces_kernel, part=part),
        place,
        [shape_of(((groups - 1) * part, width), BF)],
        *((m, True) for m in messages),
        name="pieces",
    )
    mine = list(mine) + [swap(mine[0], "wide", 2 * j) for j in (1, 2, 3)]

    merged_own, merged_sent, merged_onward = whole(
        cut_kernel,
        place,
        [
            shape_of((tokens, merged.shape[1] // 4), BF),
            shape_of((2, tokens, merged.shape[1] // 4), BF),
            shape_of((tokens, merged.shape[1] // 4), BF),
        ],
        (arrange(merged, "hqcn"), True),
        name="cut",
    )
    normed1_cut = arrange(normed1, "hqcn")

    positions = jnp.arange(KEY_ROWS)
    extent = lax.dynamic_slice_in_dim(window_extent, rank * windows, windows, 0)
    valid = (
        (positions[None, :] // WIN < extent[:, 0:1])
        & (positions[None, :] % WIN < extent[:, 1:2])
        & (positions[None, :] < WINDOW_TOKENS)
    )
    mask = jnp.where(valid, 0.0, -1e30).astype(F32)[:, None, :]
    bias = whole(
        functools.partial(spread_kernel, part=part, groups=groups),
        place,
        [shape_of((QUERY_ROWS * heads, KEY_ROWS), F32)],
        (message, True),
        *((m, True) for m in messages),
        scratch=[pltpu.VMEM((heads, OFFSETS), F32)],
        name="spread",
    )[0]
    heads_out, probs = whole(
        functools.partial(attend_kernel, windows=windows, head_dim=head_dim),
        place,
        [
            shape_of((tokens, width), BF),
            shape_of((PROBS_ROOM, windows, heads // 4, QUERY_ROWS, KEY_ROWS), F32),
        ],
        (qkv, True), (bias, True), (mask, True),
        leave=(1,),
        scratch=[
            pltpu.VMEM((4, windows, heads // 4, QUERY_ROWS, KEY_ROWS), F32),
            pltpu.SemaphoreType.DMA((4,)),
        ],
        name="attend",
    )

    mine = whole(
        mine_kernel,
        place,
        [shape_of((4 * mine[0].shape[0], width), BF)],
        *((m, True) for m in mine),
        after=(heads_out,),
        name="mine",
    )[0]
    theirs = swap(mine, "wide", 1)
    resid1, normed2, merged_sent, normed1_cut, merged_onward = whole(
        functools.partial(after_kernel, groups=groups),
        place,
        [shape_of((tokens, width), F32), shape_of((tokens, width), BF)],
        (heads_out, True), (resid0, True),
        (row(proj_bias), True), (row(norm2_gain), True), (row(norm2_shift), True),
        (proj_weight, True), (mine, True), (theirs, True),
        scratch=[pltpu.VMEM((width, width), BF)],
        through=(merged_sent, normed1_cut, merged_onward),
        name="after",
    )
    merged_near = swap(merged_sent, "wide", 4)
    normed1_near = swap(normed1_cut, "wide", 2)
    blocks = [normed2] + [turn(normed2, "narrow", step) for step in range(1, groups)]

    merged_onward = jnp.stack([merged_onward, merged_near[1]])
    merged_far = swap(merged_onward, "wide", 2)
    normed1_both = jnp.stack([normed1_cut, normed1_near])
    normed1_far = swap(normed1_both, "wide", 4)

    total, units = groups * pad, fc1_weight.shape[1]
    dy_rows, dy_own, d_act = whole(
        functools.partial(slope_kernel, groups=groups, pad=pad, chunk=256),
        place,
        [
            shape_of((total, width), BF),
            shape_of((tokens, width), BF),
            shape_of((total, units), F32),
        ],
        (out_grad, True), (fc2_weight, True),
        scratch=[pltpu.VMEM(out_grad.shape, F32)],
        after=(normed2,),
        name="slope",
    )
    act, d_pre, rows_all, fc1_b_grad, *chunks = whole(
        functools.partial(feed_kernel, pad=pad, chunk=256),
        place,
        [
            shape_of((total, units), BF),
            shape_of((total, units), BF),
            shape_of((total, width), BF),
            shape_of((1, units), F32),
        ]
        + [shape_of((tokens, width), BF)] * 4,
        *((b, True) for b in blocks), (d_act, True), (fc1_weight, True), (row(fc1_bias), True),
        after=(normed1_far, merged_far),
        name="feed",
    )
    arrived = [chunks[0]] + [turn(chunks[j], "narrow", -j) for j in range(1, groups)]

    fc1_kept, fc1_sent = grad_call(place, [arrange(rows_all, "hqc")], [d_pre], 256, 128, "fc1_grad")
    fc2_kept, fc2_sent = grad_call(place, [arrange(act, "hqc")], [dy_rows], 256, 128, "fc2_grad")
    fc1_come, fc2_come = swap(fc1_sent, "wide", 1), swap(fc2_sent, "wide", 1)
    fc1_kept, fc1_sent = join_call(
        place, [(fc1_kept, fc1_come)],
        [
            (F32, [lambda p, y=y: (0, 2 * y + p[2] % 2, 0, 128) for y in range(2)]),
            (BF, [lambda p, y=y: (0, 2 * y + 1 - p[2] % 2, 0, 128) for y in range(2)]),
        ],
        "fc1_join",
    )
    fc2_kept, fc2_sent = join_call(
        place, [(fc2_kept, fc2_come)],
        [
            (F32, [lambda p, x=x: (0, 2 * (p[2] // 2) + x, 0, 128) for x in range(2)]),
            (BF, [lambda p, x=x: (0, 2 * (1 - p[2] // 2) + x, 0, 128) for x in range(2)]),
        ],
        "fc2_join",
    )
    fc1_come, fc2_come = swap(fc1_sent, "wide", 2), swap(fc2_sent, "wide", 4)
    fc1_kept, fc1_sent = join_call(
        place, [(fc1_kept, fc1_come)],
        [
            (F32, [lambda p: (0, p[2] // 2, 0, 128)]),
            (BF, [lambda p: (0, 1 - p[2] // 2, 0, 128)]),
        ],
        "fc1_join2",
    )
    fc2_kept, fc2_sent = join_call(
        place, [(fc2_kept, fc2_come)],
        [
            (F32, [lambda p: (0, p[2] % 2, 0, 128)]),
            (BF, [lambda p: (0, 1 - p[2] % 2, 0, 128)]),
        ],
        "fc2_join2",
    )
    fc1_come, fc2_come = swap(fc1_sent, "wide", 4), swap(fc2_sent, "wide", 2)
    second_kept, second_sent = whole(
        functools.partial(second_kernel, pad=pad, groups=groups),
        place,
        [shape_of((2, tokens, width), BF)] * 2,
        (act, True),
        (fc2_weight, True),
        name="second",
    )
    d_resid1, d_heads, second_sent = whole(
        functools.partial(back2_kernel, groups=groups),
        place,
        [shape_of((tokens + 8, width), F32), shape_of((tokens, width), BF)],
        *((a, True) for a in arrived),
        (resid1, True), (dy_own, True), (row(norm2_gain), True),
        (proj_weight, True), (mine, True), (theirs, True),
        scratch=[pltpu.VMEM((width, width), BF)],
        after=(fc1_sent, fc2_sent),
        through=(second_sent,),
        name="back2",
    )
    second_come = swap(second_sent, "narrow", 1)
    *d_parts, rel_part = whole(
        functools.partial(attend_back_kernel, windows=windows, head_dim=head_dim),
        place,
        [shape_of((tokens, 3 * width // 4), BF)] * 4 + [shape_of((heads, OFFSETS), F32)],
        (qkv, True), (d_heads, True), (probs, False),
        scratch=[
            pltpu.VMEM((QUERY_ROWS * heads, KEY_ROWS), F32),
            pltpu.VMEM((4, *probs.shape[1:]), F32),
            pltpu.SemaphoreType.DMA((4,)),
        ],
        after=(fc1_come, fc2_come),
        name="attend_back",
    )
    d_come = [swap(d_parts[j], "wide", 2 * j) for j in (1, 2, 3)]

    d_resid0, sums1 = whole(
        back1_kernel,
        place,
        [shape_of((tokens, width), BF), shape_of((5, width), F32)],
        *((d, True) for d in d_parts), (d_resid1, True), (resid0, True),
        (row(norm1_gain), True), (qkv_weight, False),
        scratch=[
            pltpu.VMEM((3, width, width), BF),
            pltpu.SemaphoreType.DMA((3,)),
        ],
        name="back1",
    )
    d_flat, sums0 = whole(
        back0_kernel,
        place,
        [shape_of(flat.shape, BF), shape_of((2 * flat.shape[1] // width, width), F32)],
        (d_resid0, True), (flat, True), (row(merge_gain), True), (merge_weight, False),
        scratch=[pltpu.VMEM(merge_weight.shape, BF), pltpu.SemaphoreType.DMA((1,))],
        name="back0",
    )

    second_own, second_sent = join_call(
        place, [(second_kept, second_come)],
        [(F32, [lambda p: (0, 0, 0, tokens)]), (BF, [lambda p: (0, 1, 0, tokens)])],
        "second_join",
    )
    second_come = swap(second_sent, "narrow", 2)

    proj_kept, proj_sent = grad_call(
        place, [arrange(heads_out, "nhqc")], [d_resid1], 256, 32, "proj_grad", after=(d_resid0,)
    )
    proj_come = swap(proj_sent, "wide", 1)

    side = lambda pick_x: [
        lambda p, n=n, y=y: (0, n, (2 * y + pick_x(p[2] % 2)) * 32, 32)
        for n in range(groups) for y in range(2)
    ]
    proj_kept, proj_sent = join_call(
        place, [(proj_kept, proj_come)],
        [(F32, side(lambda x: x)), (BF, side(lambda x: 1 - x))],
        "proj_join",
    )
    proj_come = swap(proj_sent, "wide", 2)

    own_sums, d_resid0 = whole(
        collect_kernel,
        place,
        [shape_of((48, 3 * width // 4), F32)],
        (sums0, True), (sums1, True), (d_resid1, True), (rel_part, True), (fc1_b_grad, True),
        after=(*d_come, second_sent, proj_sent),
        through=(d_resid0,),
        name="collect",
    )
    r_come = [swap(d_resid0, "wide", 2 * j) for j in (1, 2, 3)]
    qkv_kept, qkv_sent = grad_call(
        place,
        [normed1_cut, (normed1_both, 1), (normed1_far, 0), (normed1_far, 1)],
        [d_parts[0], *d_come],
        256, 128, "qkv_grad", sums=own_sums, after=(second_sent,),
    )
    qkv_come = swap(qkv_sent, "wide", 1)
    rows = 128 // groups
    qkv_pieces = lambda flip: [
        lambda p, g=g, k=k: (0, g, (2 * k + (p[0] + flip) % 2) * rows, rows)
        for k in range(2) for g in range(4)
    ]
    own_sums, qkv_kept, qkv_sent = join_call(
        place, [(qkv_kept, qkv_come)], [(F32, qkv_pieces(0)), (BF, qkv_pieces(1))], "qkv_join",
        sums=(own_sums, 4),
    )
    qkv_come = swap(qkv_sent, "narrow", 1)

    merge_kept, merge_sent = grad_call(
        place,
        [merged_own, (merged_far, 0), (merged_near, 0), (merged_far, 1)],
        [d_resid0, *r_come],
        merged_own.shape[1], merged_own.shape[1] // 2, "merge_grad", after=(qkv_sent,),
    )
    merge_come = swap(merge_sent, "wide", 1)

    second_pieces = lambda flip: [
        lambda p, g=g: (0, ((p[0] // 2 + flip) % 2) * 4 + g, 0, rows) for g in range(4)
    ]
    own_sums, qkv_kept, qkv_sent = join_call(
        place, [(qkv_kept, qkv_come)],
        [(F32, second_pieces(0)), (BF, second_pieces(1))],
        "qkv_join2",
        sums=(own_sums, 8),
        after=(merge_sent,),
    )
    qkv_come = swap(qkv_sent, "narrow", 2)
    merge_rows = merged_own.shape[1] // 2 // groups
    merge_pieces = lambda flip: [
        lambda p, k=k: (0, 0, (2 * k + (p[0] + flip) % 2) * merge_rows, merge_rows)
        for k in range(2)
    ]
    merge_kept, merge_sent, fc1_come, fc2_come, d_flat = join_call(
        place, [(merge_kept, merge_come)],
        [(F32, merge_pieces(0)), (BF, merge_pieces(1))],
        "merge_join",
        after=(qkv_sent,),
        through=(fc1_come, fc2_come, d_flat),
    )
    merge_first = merge_sent
    merge_come = swap(merge_sent, "narrow", 1)

    last_pieces = lambda flip, size: [lambda p: (0, (p[0] // 2 + flip) % 2, 0, size)]
    merge_kept, merge_sent = join_call(
        place, [(merge_kept, merge_come)],
        [(F32, last_pieces(0, merge_rows)), (BF, last_pieces(1, merge_rows))],
        "merge_join2",
        after=(qkv_sent,),
    )
    merge_last = merge_sent
    merge_come = swap(merge_sent, "narrow", 2)

    proj_kept, proj_sent = join_call(
        place, [(proj_kept, proj_come)],
        [
            (F32, [lambda p, n=n: (0, 2 * n + p[2] // 2, 0, 32) for n in range(groups)]),
            (BF, [lambda p, n=n: (0, 2 * n + 1 - p[2] // 2, 0, 32) for n in range(groups)]),
        ],
        "proj_join2",
        after=(merge_first,),
    )
    proj_come = swap(proj_sent, "wide", 4)
    proj_pieces = lambda flip: [
        lambda p, k=k: (0, 2 * k + (p[0] + flip) % 2, 0, 32) for k in range(2)
    ]
    proj_kept, proj_sent = join_call(
        place, [(proj_kept, proj_come)], [(F32, proj_pieces(0)), (BF, proj_pieces(1))],
        "proj_join3",
        after=(merge_sent,),
    )
    proj_come = swap(proj_sent, "narrow", 1)
    proj_kept, proj_sent = join_call(
        place, [(proj_kept, proj_come)],
        [(F32, last_pieces(0, 32)), (BF, last_pieces(1, 32))],
        "proj_join4",
    )
    proj_come = swap(proj_sent, "narrow", 2)

    own_sums, *cuts = join_call(
        place, [(qkv_kept, qkv_come)],
        [(BF, [lambda p, j=j: (0, p[2] ^ j, 0, rows)]) for j in range(4)],
        "qkv_join3",
        sums=(own_sums, 4),
        after=(merge_last,),
    )
    cuts = [cuts[0]] + [swap(cuts[j], "wide", 2 * j) for j in (1, 2, 3)]
    qkv_out, all_sums = whole(
        columns_kernel,
        place,
        [shape_of((rows, 3 * width), F32), shape_of(own_sums.shape, F32)],
        *((c, True) for c in cuts), (own_sums, True),
        name="columns",
    )
    qkv_out = settle(qkv_out[None])
    mask = 8
    while mask < wide:
        all_sums = all_sums + swap(all_sums, "wide", mask)
        mask *= 2
    merge_out = settle(merge_kept + merge_come.astype(F32))
    proj_out = settle(proj_kept + proj_come.astype(F32))

    fc1_out = settle(fc1_kept + fc1_come.astype(F32))
    fc2_out = settle(fc2_kept + fc2_come.astype(F32))
    patches_grad = d_flat.reshape(patches.shape)
    output = low(resid1 + row(fc2_bias) + second_own[0] + second_come[0].astype(F32))

    deep = merged.shape[1]
    *vectors, rel_grad, fc1_b_mine = whole(
        functools.partial(deliver_kernel, heads=heads),
        place,
        [
            shape_of((size,), F32)
            for size in (deep, deep, width, width, 3 * width, width, width, width, width)
        ]
        + [shape_of((heads, rel_table.shape[0]), F32), shape_of((units // 128, 128), F32)],
        (all_sums, True),
        name="deliver",
    )
    fc1_b_out = lax.dynamic_index_in_dim(
        fc1_b_mine.reshape(wide, -1), wide_at, 0, keepdims=False
    )

    return (
        output,
        patches_grad,
        vectors[0],
        vectors[1],
        merge_out,
        vectors[2],
        vectors[3],
        qkv_out,
        vectors[4],
        jnp.transpose(rel_grad),
        proj_out,
        vectors[5],
        vectors[6],
        vectors[7],
        fc1_out,
        fc1_b_out,
        fc2_out,
        vectors[8],
    )


def solution(mesh):
    in_specs = (
        P(("wide", "narrow"), None, None),
        P("wide", None),
        P(),
        P(),
        P(),
        P(),
        P(),
        P(),
        P(),
        P(None, "narrow"),
        P("narrow", None),
        P(),
        P(),
        P(),
        P(None, "narrow"),
        P("narrow"),
        P("narrow", None),
        P(),
        P("wide", None),
    )
    out_specs = (
        P(("wide", "narrow"), None),
        P(("wide", "narrow"), None, None),
        P(),
        P(),
        P(("wide", "narrow"), None),
        P(),
        P(),
        P(("wide", "narrow"), None),
        P(),
        P(),
        P(("narrow", "wide"), None),
        P(),
        P(),
        P(),
        P("wide", "narrow"),
        P(("narrow", "wide")),
        P(("narrow", "wide"), None),
        P(),
    )
    return jax.shard_map(
        on_device, mesh=mesh, in_specs=in_specs, out_specs=out_specs, check_vma=False
    )
```

profile of v0, /device:TPU:0, one launch (start us, length us, event | category | flops | bytes accessed | tf_op | source)
XLA Modules:
  0.0 228.8 jit_solution(5383103464200060013)
XLA Ops:
  3.3 5.1 %collective-permute-start.2 = (bf16[48,1024]{1,0:T(8,128)(2,1)S(1)}, bf16[48,1024]{1,0:T(8,128)(2,1)S(1)}, u32[]{:S(2)}, u32[]{:S(2)}) collective-permute-start(bf16[48,1024]{1,0:T(8,128)(2,1)S(1)} %pack.1.refs_0_), channel_id=1, source_target_pairs={{0,3},{1,0},{2,1},{3,2},{4,7},{5,4},{6,5},{7,6},{8,11},{9,8},{10,9... | collective-permute-start | bytes 294920 | tf_op jit(solution)/shard_map/ppermute | solution.py:127
  9.8 3.0 %copy-done.10 = bf16[1024,3072]{1,0:T(8,128)(2,1)S(1)} copy-done((bf16[1024,3072]{1,0:T(8,128)(2,1)S(1)}, bf16[1024,3072]{1,0:T(8,128)(2,1)}, u32[]{:S(2)}) %copy-start.10) | copy-done | bytes 6291480
  15.0 4.7 %front.1 = (bf16[200,2048]{1,0:T(8,128)(2,1)S(1)}, f32[200,1024]{1,0:T(8,128)S(1)}, bf16[200,1024]{1,0:T(8,128)(2,1)S(1)}, bf16[200,3072]{1,0:T(8,128)(2,1)S(1)}) custom-call(s32[3]{0:T(128)S(1)} %pad_add_fusion.place_ref, bf16[200,2048]{1,0:T(8,128)(2,1)S(1)} %bitcast.39, f32[1,2048]{1,0:T(1,128)S(1)} %bitcast.47, f32[1,2048]{1,0:T(1,128)S(1)} %bitcast.46, ...), custom_call_target="tpu_custom_call" | custom-call | flops 99999997952 | tf_op jit(solution)/shard_map/front/pallas_call | solution.py:88
  26.2 6.8 %attend.1 = (bf16[200,1024]{1,0:T(8,128)(2,1)S(1)}, f32[52,2,8,112,128]{4,3,2,1,0:T(8,128)}) custom-call(s32[3]{0:T(128)S(1)} %pad_add_fusion.place_ref, bf16[200,3072]{1,0:T(8,128)(2,1)S(1)} %get-tuple-element.118.refs_0_, f32[3584,128]{1,0:T(8,128)S(1)} %spread.1.refs_1_, f32[2,1,128]{2,1,0:T(1,128)S(1)} %and_select_fusion.refs_2_), custom_call_target="tpu_custom_call" | custom-call | flops 99999997952 | tf_op jit(solution)/shard_map/attend/pallas_call | solution.py:88
  41.5 2.8 %collective-permute-start.9 = (bf16[200,1024]{1,0:T(8,128)(2,1)S(1)}, bf16[200,1024]{1,0:T(8,128)(2,1)S(1)}, u32[]{:S(2)}, u32[]{:S(2)}) collective-permute-start(bf16[200,1024]{1,0:T(8,128)(2,1)S(1)} %get-tuple-element.126.refs_2_.refs_0_), channel_id=1, source_target_pairs={{0,3},{1,0},{2,1},{3,2},{4,7},{5,4},{6,5},{7,6},{8,11},{9,8},{10,9... | collective-permute-start | bytes 1228808 | tf_op jit(solution)/shard_map/ppermute | solution.py:127
  45.5 4.5 %collective-permute-done.12.refs_2_ = bf16[2,200,512]{2,1,0:T(8,128)(2,1)S(1)} collective-permute-done((bf16[2,200,512]{2,1,0:T(8,128)(2,1)S(1)}, bf16[2,200,512]{2,1,0:T(8,128)(2,1)S(1)}, u32[]{:S(2)}, u32[]{:S(2)}) %collective-permute-start.12) | collective-permute-done | bytes 409632 | tf_op jit(solution)/shard_map/ppermute | solution.py:122
  54.1 3.5 %slope.1 = (bf16[832,1024]{1,0:T(8,128)(2,1)S(1)}, bf16[200,1024]{1,0:T(8,128)(2,1)S(1)}, f32[832,1024]{1,0:T(8,128)S(1)}) custom-call(s32[3]{0:T(128)S(1)} %pad_add_fusion.place_ref, bf16[800,1024]{1,0:T(8,128)(2,1)S(1)} %copy-done.15, bf16[1024,1024]{1,0:T(8,128)(2,1)S(1)} %copy-done.14, bf16[200,1024]{1,0:T(8,128)(2,1)S(1)} %get-tuple-element.126.refs_2_.refs_0_), custom_call_target="tpu_custom_call" | custom-call | flops 99999997952 | tf_op jit(solution)/shard_map/slope/pallas_call | solution.py:88
  57.7 23.0 %collective-permute-done.8.refs_2_ = bf16[200,1024]{1,0:T(8,128)(2,1)S(1)} collective-permute-done((bf16[200,1024]{1,0:T(8,128)(2,1)S(1)}, bf16[200,1024]{1,0:T(8,128)(2,1)S(1)}, u32[]{:S(2)}, u32[]{:S(2)}) %collective-permute-start.8) | collective-permute-done | bytes 409632 | tf_op jit(solution)/shard_map/ppermute | solution.py:127
  80.8 8.0 %feed.1 = (bf16[832,1024]{1,0:T(8,128)(2,1)S(1)}, bf16[832,1024]{1,0:T(8,128)(2,1)S(1)}, bf16[832,1024]{1,0:T(8,128)(2,1)S(1)}, f32[1,1024]{1,0:T(1,128)S(1)}, b...) custom-call(s32[3]{0:T(128)S(1)} %pad_add_fusion.place_ref, ...), custom_call_target="tpu_custom_call" | custom-call | flops 99999997952 | tf_op jit(solution)/shard_map/feed/pallas_call | solution.py:88
  92.1 2.5 %second.1 = (bf16[2,200,1024]{2,1,0:T(8,128)(2,1)S(1)}, bf16[2,200,1024]{2,1,0:T(8,128)(2,1)S(1)}) custom-call(s32[3]{0:T(128)S(1)} %pad_add_fusion.place_ref, bf16[832,1024]{1,0:T(8,128)(2,1)S(1)} %get-tuple-element.131.refs_0_, bf16[1024,1024]{1,0:T(8,128)(2,1)S(1)} %copy-done.14), custom_call_target="tpu_custom_call" | custom-call | flops 99999997952 | tf_op jit(solution)/shard_map/second/pallas_call | solution.py:88
  94.6 4.0 %fc2_grad.1 = (f32[4,128,1024]{2,1,0:T(8,128)S(1)}, bf16[4,128,1024]{2,1,0:T(8,128)(2,1)S(1)}) custom-call(s32[3]{0:T(128)S(1)} %pad_add_fusion.place_ref, bf16[832,1024]{1,0:T(8,128)(2,1)S(1)} %get-tuple-element.131.refs_0_, bf16[832,1024]{1,0:T(8,128)(2,1)S(1)} %get-tuple-element.145.refs_1_), custom_call_target="tpu_custom_call" | custom-call | flops 99999997952 | tf_op jit(solution)/shard_map/fc2_grad/pallas_call | solution.py:88
  98.7 3.8 %fc1_grad.1 = (f32[4,128,1024]{2,1,0:T(8,128)S(1)}, bf16[4,128,1024]{2,1,0:T(8,128)(2,1)S(1)}) custom-call(s32[3]{0:T(128)S(1)} %pad_add_fusion.place_ref, bf16[832,1024]{1,0:T(8,128)(2,1)S(1)} %get-tuple-element.138.refs_0_, bf16[832,1024]{1,0:T(8,128)(2,1)S(1)} %get-tuple-element.139.refs_1_), custom_call_target="tpu_custom_call" | custom-call | flops 99999997952 | tf_op jit(solution)/shard_map/fc1_grad/pallas_call | solution.py:88
  106.7 11.0 %collective-permute-done.20.refs_1_ = bf16[2,128,1024]{2,1,0:T(8,128)(2,1)S(1)} collective-permute-done((bf16[2,128,1024]{2,1,0:T(8,128)(2,1)S(1)}, bf16[2,128,1024]{2,1,0:T(8,128)(2,1)S(1)}, u32[]{:S(2)}, u32[]{:S(2)}) %collective-permute-start.20) | collective-permute-done | bytes 524320 | tf_op jit(solution)/shard_map/ppermute | solution.py:122
  122.3 3.3 %collective-permute-done.15.refs_2_ = bf16[200,1024]{1,0:T(8,128)(2,1)} collective-permute-done((bf16[200,1024]{1,0:T(8,128)(2,1)}, bf16[200,1024]{1,0:T(8,128)(2,1)}, u32[]{:S(2)}, u32[]{:S(2)}) %collective-permute-start.15) | collective-permute-done | bytes 409632 | tf_op jit(solution)/shard_map/ppermute | solution.py:127
  125.7 3.1 %back2.1 = (f32[208,1024]{1,0:T(8,128)S(1)}, bf16[200,1024]{1,0:T(8,128)(2,1)S(1)}, bf16[2,200,1024]{2,1,0:T(8,128)(2,1)S(1)}) custom-call(s32[3]{0:T(128)S(1)} %pad_add_fusion.place_ref, bf16[200,1024]{1,0:T(8,128)(2,1)S(1)} %get-tuple-element.133.refs_0_, bf16[200,1024]{1,0:T(8,128)(2,1)} %collective-permute-done.14.refs_1_, ...), custom_call_target="tpu_custom_call", output_to_operand_aliasing={{2}: (13, {})} | custom-call | flops 5000000000 | tf_op jit(solution)/shard_map/back2/pallas_call | solution.py:88
  129.7 9.6 %attend_back.1 = (bf16[200,768]{1,0:T(8,128)(2,1)S(1)}, bf16[200,768]{1,0:T(8,128)(2,1)S(1)}, bf16[200,768]{1,0:T(8,128)(2,1)S(1)}, bf16[200,768]{1,0:T(8,128)(2,1)S(1)}, f32[32,384]{1,0:T(8,128)S(1)}) custom-call(s32[3]{0:T(128)S(1)} %pad_add_fusion.place_ref, bf16[200,3072]{1,0:T(8,128)(2,1)S(1)} %get-tuple-element.118.refs_0_, ...), custom_call_target="tpu_custom_call" | custom-call | flops 5000000000 | tf_op jit(solution)/shard_map/attend_back/pallas_call | solution.py:88
  142.9 4.2 %back1.1 = (bf16[200,1024]{1,0:T(8,128)(2,1)S(1)}, f32[5,1024]{1,0:T(8,128)S(1)}) custom-call(s32[3]{0:T(128)S(1)} %pad_add_fusion.place_ref, bf16[200,768]{1,0:T(8,128)(2,1)S(1)} %get-tuple-element.158.refs_0_.refs_4_, bf16[200,768]{1,0:T(8,128)(2,1)S(1)} %get-tuple-element.159.refs_1_, bf16[200,768]{1,0:T(8,128)(2,1)S(1)} %get-tuple-element.160.refs_2_, ...), custom_call_target="tpu_custom_call" | custom-call | flops 20000000000 | tf_op jit(solution)/shard_map/back1/pallas_call | solution.py:88
  147.1 3.4 %back0.1 = (bf16[200,2048]{1,0:T(8,128)(2,1)S(1)}, f32[4,1024]{1,0:T(4,128)S(1)}) custom-call(s32[3]{0:T(128)S(1)} %pad_add_fusion.place_ref, bf16[200,1024]{1,0:T(8,128)(2,1)S(1)} %get-tuple-element.163.refs_0_.refs_2_.refs_10_, bf16[200,2048]{1,0:T(8,128)(2,1)S(1)} %bitcast.40, f32[1,2048]{1,0:T(1,128)S(1)} %bitcast.48, bf16[2048,1024]{1,0:T(8,128)(2,1)S(1)} %copy-done.12), custom_call_target="tpu_custom_call" | custom-call | flops 20000000000 | tf_op jit(solution)/shard_map/back0/pallas_call | solution.py:88
  157.8 4.5 %qkv_grad.1 = (f32[4,128,768]{2,1,0:T(8,128)S(1)}, bf16[5,128,768]{2,1,0:T(8,128)(2,1)}) custom-call(s32[3]{0:T(128)S(1)} %pad_add_fusion.place_ref, bf16[200,1024]{1,0:T(8,128)(2,1)S(1)} %get-tuple-element.128.refs_0_, bf16[2,200,1024]{2,1,0:T(8,128)(2,1)S(1)} %copy-done.5, bf16[2,200,1024]{2,1,0:T(8,128)(2,1)S(1)} %collective-permute-done.11.refs_7_.refs_2_.refs_3_, ...), custom_call_target="tpu_custom_call" | custom-call | flops 5000000000 | tf_op jit(solution)/shard_map/qkv_grad/pallas_call | solution.py:88
  173.2 5.6 %collective-permute-done.31.refs_7_ = bf16[200,1024]{1,0:T(8,128)(2,1)S(1)} collective-permute-done((bf16[200,1024]{1,0:T(8,128)(2,1)}, bf16[200,1024]{1,0:T(8,128)(2,1)S(1)}, u32[]{:S(2)}, u32[]{:S(2)}) %collective-permute-start.31) | collective-permute-done | bytes 409632 | tf_op jit(solution)/shard_map/ppermute | solution.py:122
  178.8 7.1 %collective-permute-done.30.refs_6_ = bf16[200,1024]{1,0:T(8,128)(2,1)S(1)} collective-permute-done((bf16[200,1024]{1,0:T(8,128)(2,1)}, bf16[200,1024]{1,0:T(8,128)(2,1)S(1)}, u32[]{:S(2)}, u32[]{:S(2)}) %collective-permute-start.30) | collective-permute-done | bytes 409632 | tf_op jit(solution)/shard_map/ppermute | solution.py:122
  190.3 2.8 %collective-permute-done.34.refs_1_ = bf16[10,32,768]{2,1,0:T(8,128)(2,1)S(1)} collective-permute-done((bf16[10,32,768]{2,1,0:T(8,128)(2,1)S(1)}, bf16[10,32,768]{2,1,0:T(8,128)(2,1)S(1)}, u32[]{:S(2)}, u32[]{:S(2)}) %collective-permute-start.34) | collective-permute-done | bytes 491552 | tf_op jit(solution)/shard_map/ppermute | solution.py:122
  198.8 4.6 %collective-permute-done.41.refs_1_ = bf16[8,32,1024]{2,1,0:T(8,128)(2,1)S(1)} collective-permute-done((bf16[8,32,1024]{2,1,0:T(8,128)(2,1)S(1)}, bf16[8,32,1024]{2,1,0:T(8,128)(2,1)S(1)}, u32[]{:S(2)}, u32[]{:S(2)}) %collective-permute-start.41) | collective-permute-done | bytes 524320 | tf_op jit(solution)/shard_map/ppermute | solution.py:122
  211.7 3.0 %collective-permute-done.42.refs_1_ = bf16[4,32,1024]{2,1,0:T(8,128)(2,1)S(1)} collective-permute-done((bf16[4,32,1024]{2,1,0:T(8,128)(2,1)}, bf16[4,32,1024]{2,1,0:T(8,128)(2,1)S(1)}, u32[]{:S(2)}, u32[]{:S(2)}) %collective-permute-start.42) | collective-permute-done | bytes 262176 | tf_op jit(solution)/shard_map/ppermute | solution.py:122
  (250 shorter events, 93.1 us)
Async XLA Ops:
  3.3 16.5 %collective-permute-start.2 = (bf16[48,1024]{1,0:T(8,128)(2,1)S(1)}, bf16[48,1024]{1,0:T(8,128)(2,1)S(1)}, u32[]{:S(2)}, u32[]{:S(2)}) collective-permute-start(bf16[48,1024]{1,0:T(8,128)(2,1)S(1)} %pack.1.refs_0_), channel_id=1, source_target_pairs={{0,3},{1,0},{2,1},{3,2},{4,7},{5,4},{6,5},{7,6},{8,11},{9,8},{10,9... | collective-permute-start | bytes 294920 | tf_op jit(solution)/shard_map/ppermute | solution.py:127
  40.1 12.4 %collective-permute-start.10 = (bf16[200,1024]{1,0:T(8,128)(2,1)S(1)}, bf16[200,1024]{1,0:T(8,128)(2,1)S(1)}, u32[]{:S(2)}, u32[]{:S(2)}) collective-permute-start(bf16[200,1024]{1,0:T(8,128)(2,1)S(1)} %get-tuple-element.128.refs_0_), channel_id=1, source_target_pairs={{0,8},{4,12},{8,0},{12,4},{16,24},{20,28},{24,16},{28,20},{1,9},{5... | collective-permute-start | bytes 1228808 | tf_op jit(solution)/shard_map/ppermute | solution.py:122
  41.5 16.1 %collective-permute-start.9 = (bf16[200,1024]{1,0:T(8,128)(2,1)S(1)}, bf16[200,1024]{1,0:T(8,128)(2,1)S(1)}, u32[]{:S(2)}, u32[]{:S(2)}) collective-permute-start(bf16[200,1024]{1,0:T(8,128)(2,1)S(1)} %get-tuple-element.126.refs_2_.refs_0_), channel_id=1, source_target_pairs={{0,3},{1,0},{2,1},{3,2},{4,7},{5,4},{6,5},{7,6},{8,11},{9,8},{10,9... | collective-permute-start | bytes 1228808 | tf_op jit(solution)/shard_map/ppermute | solution.py:127
  44.4 36.4 %collective-permute-start.8 = (bf16[200,1024]{1,0:T(8,128)(2,1)S(1)}, bf16[200,1024]{1,0:T(8,128)(2,1)S(1)}, u32[]{:S(2)}, u32[]{:S(2)}) collective-permute-start(bf16[200,1024]{1,0:T(8,128)(2,1)S(1)} %get-tuple-element.126.refs_2_.refs_0_), channel_id=1, source_target_pairs={{0,2},{1,3},{2,0},{3,1},{4,6},{5,7},{6,4},{7,5},{8,10},{9,11},{10,... | collective-permute-start | bytes 1228808 | tf_op jit(solution)/shard_map/ppermute | solution.py:127
  45.5 35.3 %collective-permute-start.7 = (bf16[200,1024]{1,0:T(8,128)(2,1)S(1)}, bf16[200,1024]{1,0:T(8,128)(2,1)S(1)}, u32[]{:S(2)}, u32[]{:S(2)}) collective-permute-start(bf16[200,1024]{1,0:T(8,128)(2,1)S(1)} %get-tuple-element.126.refs_2_.refs_0_), channel_id=1, source_target_pairs={{0,1},{1,2},{2,3},{3,0},{4,5},{5,6},{6,7},{7,4},{8,9},{9,10},{10,1... | collective-permute-start | bytes 1228808 | tf_op jit(solution)/shard_map/ppermute | solution.py:127
  50.9 29.9 %collective-permute-start.13 = (bf16[2,200,512]{2,1,0:T(8,128)(2,1)S(1)}, bf16[2,200,512]{2,1,0:T(8,128)(2,1)S(1)}, u32[]{:S(2)}, u32[]{:S(2)}) collective-permute-start(bf16[2,200,512]{2,1,0:T(8,128)(2,1)S(1)} %pad_maximum_fusion.1), channel_id=1, source_target_pairs={{0,8},{4,12},{8,0},{12,4},{16,24},{20,28},{24,16},{28,20},{1,9},{5... | collective-permute-start | bytes 1228808 | tf_op jit(solution)/shard_map/ppermute | solution.py:122
  52.6 28.2 %collective-permute-start.11 = (bf16[2,200,1024]{2,1,0:T(8,128)(2,1)S(1)}, bf16[2,200,1024]{2,1,0:T(8,128)(2,1)S(1)}, u32[]{:S(2)}, u32[]{:S(2)}) collective-permute-start(bf16[2,200,1024]{2,1,0:T(8,128)(2,1)S(1)} %pad_maximum_fusion.refs_1_), channel_id=1, source_target_pairs={{0,16},{4,20},{8,24},{12,28},{16,0},{20,4},{24,8},{28,12},{1,17},{... | collective-permute-start | bytes 2457608 | tf_op jit(solution)/shard_map/ppermute | solution.py:122
  88.8 33.5 %collective-permute-start.14 = (bf16[200,1024]{1,0:T(8,128)(2,1)}, bf16[200,1024]{1,0:T(8,128)(2,1)}, u32[]{:S(2)}, u32[]{:S(2)}) collective-permute-start(bf16[200,1024]{1,0:T(8,128)(2,1)} %get-tuple-element.134), channel_id=1, source_target_pairs={{0,3},{1,0},{2,1},{3,2},{4,7},{5,4},{6,5},{7,6},{8,11},{9,8},{10,9... | collective-permute-start | bytes 1228808 | tf_op jit(solution)/shard_map/ppermute | solution.py:127
  88.8 36.8 %collective-permute-start.15 = (bf16[200,1024]{1,0:T(8,128)(2,1)}, bf16[200,1024]{1,0:T(8,128)(2,1)}, u32[]{:S(2)}, u32[]{:S(2)}) collective-permute-start(bf16[200,1024]{1,0:T(8,128)(2,1)} %get-tuple-element.135), channel_id=1, source_target_pairs={{0,2},{1,3},{2,0},{3,1},{4,6},{5,7},{6,4},{7,5},{8,10},{9,11},{10,... | collective-permute-start | bytes 1228808 | tf_op jit(solution)/shard_map/ppermute | solution.py:127
  90.0 35.6 %collective-permute-start.16 = (bf16[200,1024]{1,0:T(8,128)(2,1)}, bf16[200,1024]{1,0:T(8,128)(2,1)}, u32[]{:S(2)}, u32[]{:S(2)}) collective-permute-start(bf16[200,1024]{1,0:T(8,128)(2,1)} %get-tuple-element.136), channel_id=1, source_target_pairs={{0,1},{1,2},{2,3},{3,0},{4,5},{5,6},{6,7},{7,4},{8,9},{9,10},{10,1... | collective-permute-start | bytes 1228808 | tf_op jit(solution)/shard_map/ppermute | solution.py:127
  103.8 13.9 %collective-permute-start.20 = (bf16[2,128,1024]{2,1,0:T(8,128)(2,1)S(1)}, bf16[2,128,1024]{2,1,0:T(8,128)(2,1)S(1)}, u32[]{:S(2)}, u32[]{:S(2)}) collective-permute-start(bf16[2,128,1024]{2,1,0:T(8,128)(2,1)S(1)} %get-tuple-element.149), channel_id=1, source_target_pairs={{0,16},{4,20},{8,24},{12,28},{16,0},{20,4},{24,8},{28,12},{1,17},{... | collective-permute-start | bytes 1572872 | tf_op jit(solution)/shard_map/ppermute | solution.py:122
  106.1 14.3 %collective-permute-start.18 = (bf16[2,128,1024]{2,1,0:T(8,128)(2,1)S(1)}, bf16[2,128,1024]{2,1,0:T(8,128)(2,1)S(1)}, u32[]{:S(2)}, u32[]{:S(2)}) collective-permute-start(bf16[2,128,1024]{2,1,0:T(8,128)(2,1)S(1)} %get-tuple-element.143), channel_id=1, source_target_pairs={{0,8},{4,12},{8,0},{12,4},{16,24},{20,28},{24,16},{28,20},{1,9},{5... | collective-permute-start | bytes 1572872 | tf_op jit(solution)/shard_map/ppermute | solution.py:122
  128.8 23.9 %collective-permute-start.21 = (bf16[2,200,1024]{2,1,0:T(8,128)(2,1)S(1)}, bf16[2,200,1024]{2,1,0:T(8,128)(2,1)S(1)}, u32[]{:S(2)}, u32[]{:S(2)}) collective-permute-start(bf16[2,200,1024]{2,1,0:T(8,128)(2,1)S(1)} %get-tuple-element.152), channel_id=1, source_target_pairs={{0,1},{1,0},{2,3},{3,2},{4,5},{5,4},{6,7},{7,6},{8,9},{9,8},{10,11... | collective-permute-start | bytes 2457608 | tf_op jit(solution)/shard_map/ppermute | solution.py:122
  139.3 16.8 %collective-permute-start.25 = (bf16[200,768]{1,0:T(8,128)(2,1)S(1)}, bf16[200,768]{1,0:T(8,128)(2,1)S(1)}, u32[]{:S(2)}, u32[]{:S(2)}) collective-permute-start(bf16[200,768]{1,0:T(8,128)(2,1)S(1)} %get-tuple-element.159.refs_1_), channel_id=1, source_target_pairs={{0,8},{4,12},{8,0},{12,4},{16,24},{20,28},{24,16},{28,20},{1,9},{5... | collective-permute-start | bytes 921608 | tf_op jit(solution)/shard_map/ppermute | solution.py:122
  139.9 16.2 %collective-permute-start.26 = (bf16[200,768]{1,0:T(8,128)(2,1)S(1)}, bf16[200,768]{1,0:T(8,128)(2,1)S(1)}, u32[]{:S(2)}, u32[]{:S(2)}) collective-permute-start(bf16[200,768]{1,0:T(8,128)(2,1)S(1)} %get-tuple-element.160.refs_2_), channel_id=1, source_target_pairs={{0,16},{4,20},{8,24},{12,28},{16,0},{20,4},{24,8},{28,12},{1,17},{... | collective-permute-start | bytes 921608 | tf_op jit(solution)/shard_map/ppermute | solution.py:122
  140.4 15.7 %collective-permute-start.27 = (bf16[200,768]{1,0:T(8,128)(2,1)S(1)}, bf16[200,768]{1,0:T(8,128)(2,1)S(1)}, u32[]{:S(2)}, u32[]{:S(2)}) collective-permute-start(bf16[200,768]{1,0:T(8,128)(2,1)S(1)} %get-tuple-element.161.refs_3_), channel_id=1, source_target_pairs={{0,24},{4,28},{8,16},{12,20},{16,8},{20,12},{24,0},{28,4},{1,25},{... | collective-permute-start | bytes 921608 | tf_op jit(solution)/shard_map/ppermute | solution.py:122
  163.6 24.4 %collective-permute-start.22 = (bf16[1,200,1024]{2,1,0:T(8,128)(2,1)}, bf16[1,200,1024]{2,1,0:T(8,128)(2,1)S(1)}, u32[]{:S(2)}, u32[]{:S(2)}) collective-permute-start(bf16[1,200,1024]{2,1,0:T(8,128)(2,1)} %copy-done.27), channel_id=1, source_target_pairs={{0,2},{1,3},{2,0},{3,1},{4,6},{5,7},{6,4},{7,5},{8,10},{9,11},{10,... | collective-permute-start | bytes 1228808 | tf_op jit(solution)/shard_map/ppermute | solution.py:122
  165.3 13.5 %collective-permute-start.31 = (bf16[200,1024]{1,0:T(8,128)(2,1)}, bf16[200,1024]{1,0:T(8,128)(2,1)S(1)}, u32[]{:S(2)}, u32[]{:S(2)}) collective-permute-start(bf16[200,1024]{1,0:T(8,128)(2,1)} %copy-done.28), channel_id=1, source_target_pairs={{0,24},{4,28},{8,16},{12,20},{16,8},{20,12},{24,0},{28,4},{1,25},{... | collective-permute-start | bytes 1228808 | tf_op jit(solution)/shard_map/ppermute | solution.py:122
  165.8 20.2 %collective-permute-start.30 = (bf16[200,1024]{1,0:T(8,128)(2,1)}, bf16[200,1024]{1,0:T(8,128)(2,1)S(1)}, u32[]{:S(2)}, u32[]{:S(2)}) collective-permute-start(bf16[200,1024]{1,0:T(8,128)(2,1)} %copy-done.28), channel_id=1, source_target_pairs={{0,16},{4,20},{8,24},{12,28},{16,0},{20,4},{24,8},{28,12},{1,17},{... | collective-permute-start | bytes 1228808 | tf_op jit(solution)/shard_map/ppermute | solution.py:122
  167.3 18.6 %collective-permute-start.29 = (bf16[200,1024]{1,0:T(8,128)(2,1)}, bf16[200,1024]{1,0:T(8,128)(2,1)S(1)}, u32[]{:S(2)}, u32[]{:S(2)}) collective-permute-start(bf16[200,1024]{1,0:T(8,128)(2,1)} %copy-done.28), channel_id=1, source_target_pairs={{0,8},{4,12},{8,0},{12,4},{16,24},{20,28},{24,16},{28,20},{1,9},{5... | collective-permute-start | bytes 1228808 | tf_op jit(solution)/shard_map/ppermute | solution.py:122
  172.6 20.5 %collective-permute-start.34 = (bf16[10,32,768]{2,1,0:T(8,128)(2,1)S(1)}, bf16[10,32,768]{2,1,0:T(8,128)(2,1)S(1)}, u32[]{:S(2)}, u32[]{:S(2)}) collective-permute-start(bf16[10,32,768]{2,1,0:T(8,128)(2,1)S(1)} %get-tuple-element.175.refs_8_), channel_id=1, source_target_pairs={{0,1},{1,0},{2,3},{3,2},{4,5},{5,4},{6,7},{7,6},{8,9},{9,8},{10,11... | collective-permute-start | bytes 1474568 | tf_op jit(solution)/shard_map/ppermute | solution.py:122
  189.0 14.3 %collective-permute-start.41 = (bf16[8,32,1024]{2,1,0:T(8,128)(2,1)S(1)}, bf16[8,32,1024]{2,1,0:T(8,128)(2,1)S(1)}, u32[]{:S(2)}, u32[]{:S(2)}) collective-permute-start(bf16[8,32,1024]{2,1,0:T(8,128)(2,1)S(1)} %copy-done.24), channel_id=1, source_target_pairs={{0,8},{4,12},{8,0},{12,4},{16,24},{20,28},{24,16},{28,20},{1,9},{5... | collective-permute-start | bytes 1572872 | tf_op jit(solution)/shard_map/ppermute | solution.py:122
  195.2 20.7 %collective-permute-start.35 = (bf16[6,32,768]{2,1,0:T(8,128)(2,1)S(1)}, bf16[6,32,768]{2,1,0:T(8,128)(2,1)S(1)}, u32[]{:S(2)}, u32[]{:S(2)}) collective-permute-start(bf16[6,32,768]{2,1,0:T(8,128)(2,1)S(1)} %get-tuple-element.180.refs_2_), channel_id=1, source_target_pairs={{0,2},{1,3},{2,0},{3,1},{4,6},{5,7},{6,4},{7,5},{8,10},{9,11},{10,... | collective-permute-start | bytes 884744 | tf_op jit(solution)/shard_map/ppermute | solution.py:122
  196.6 12.9 %collective-permute-start.36 = (bf16[2,64,1024]{2,1,0:T(8,128)(2,1)S(1)}, bf16[2,64,1024]{2,1,0:T(8,128)(2,1)S(1)}, u32[]{:S(2)}, u32[]{:S(2)}) collective-permute-start(bf16[2,64,1024]{2,1,0:T(8,128)(2,1)S(1)} %get-tuple-element.186.refs_2_), channel_id=1, source_target_pairs={{0,1},{1,0},{2,3},{3,2},{4,5},{5,4},{6,7},{7,6},{8,9},{9,8},{10,11... | collective-permute-start | bytes 786440 | tf_op jit(solution)/shard_map/ppermute | solution.py:122
  (85 other events, 537.4 us)
where the time goes:
time: 229 us
  Pallas kernels  82.3 us (36%)
  waiting for transfers between devices  76 us (33%)
  starting transfers between devices  45.3 us (20%)
  local copies, waits for them, and re-layouts  19.1 us (8%)
  other arithmetic  4.36 us (2%)
    pallas_call x37, Pallas kernels, whole(): pl.pallas_call(body, in_specs=[pl.BlockSpec(memory_space=pltpu.SMEM)] + [...  82.3 us
    ppermute x36, waiting for transfers between devices, swap(): return lax.ppermute(array, axis, [(i, i ^ mask) for i in range(size)])  49.6 us
    ppermute x36, starting transfers between devices, swap(): return lax.ppermute(array, axis, [(i, i ^ mask) for i in range(size)])  32 us
    ppermute x9, waiting for transfers between devices, turn(): lax.ppermute(array, axis, [(i, (i + step) % size) for i in range(size)])  26.4 us
    unnamed x130, local copies, waits for them, and re-layouts  17 us
    ppermute x9, starting transfers between devices, turn(): lax.ppermute(array, axis, [(i, (i + step) % size) for i in range(size)])  13.3 us
  transfers between devices with their start and end apart: 45, of which 17 were waited for; matrix products, arithmetic and copies ran while one was open for 3% of the time, Pallas kernels for 28%

commit v1 on v0

--- a/solution.py
+++ b/solution.py
@@ -574,7 +574,7 @@
     def keep(step):
         return pltpu.make_async_copy(probs_ref.at[step], probs_any.at[step], sems.at[step])
 
-    @pl.loop(0, 4)
+    @pl.loop(0, 4, unroll=True)
     def _(step):
         attend_group(
             step, qkv_ref, bias_ref, mask_ref, out_ref, probs_ref, windows, head_dim, width, lanes
@@ -741,15 +741,17 @@
 
 
 def columns_kernel(place_ref, b0_ref, b1_ref, b2_ref, b3_ref, own_ref, out_ref, sums_ref):
-    rows = out_ref.shape[0]
+    rows, step = out_ref.shape[0], b0_ref.shape[1]
     lanes = b0_ref.shape[2] // 3
     total = own_ref[...]
     for j, ref in enumerate((b0_ref, b1_ref, b2_ref, b3_ref)):
         for part in range(3):
             at = pl.multiple_of((part * 4 + (place_ref[2] ^ j)) * lanes, lanes)
-            out_ref[:, pl.ds(at, lanes)] = ref[0, :rows, part * lanes : (part + 1) * lanes].astype(F32)
+            for s in range(rows // step):
+                block = ref[s, :, part * lanes : (part + 1) * lanes].astype(F32)
+                out_ref[s * step : (s + 1) * step, pl.ds(at, lanes)] = block
         if j:
-            total = total + take_sums(ref, 1, own_ref.shape[0])
+            total = total + take_sums(ref, rows // step, own_ref.shape[0])
     sums_ref[...] = total
 
 
@@ -1070,9 +1072,11 @@
     )
     qkv_come = swap(qkv_sent, "wide", 1)
     rows = 128 // groups
+    step = 16 if rows % 16 == 0 else rows
+    cuts_of = rows // step
     qkv_pieces = lambda flip: [
-        lambda p, g=g, k=k: (0, g, (2 * k + (p[0] + flip) % 2) * rows, rows)
-        for k in range(2) for g in range(4)
+        lambda p, g=g, k=k, s=s: (0, g, (2 * k + (p[0] + flip) % 2) * rows + s * step, step)
+        for k in range(2) for g in range(4) for s in range(cuts_of)
     ]
     own_sums, qkv_kept, qkv_sent = join_call(
         place, [(qkv_kept, qkv_come)], [(F32, qkv_pieces(0)), (BF, qkv_pieces(1))], "qkv_join",
@@ -1089,13 +1093,14 @@
     merge_come = swap(merge_sent, "wide", 1)
 
     second_pieces = lambda flip: [
-        lambda p, g=g: (0, ((p[0] // 2 + flip) % 2) * 4 + g, 0, rows) for g in range(4)
+        lambda p, g=g: (0, ((p[0] // 2 + flip) % 2) * 4 * cuts_of + g, 0, step)
+        for g in range(4 * cuts_of)
     ]
     own_sums, qkv_kept, qkv_sent = join_call(
         place, [(qkv_kept, qkv_come)],
         [(F32, second_pieces(0)), (BF, second_pieces(1))],
         "qkv_join2",
-        sums=(own_sums, 8),
+        sums=(own_sums, 8 * cuts_of),
         after=(merge_sent,),
     )
     qkv_come = swap(qkv_sent, "narrow", 2)
@@ -1152,9 +1157,12 @@
 
     own_sums, *cuts = join_call(
         place, [(qkv_kept, qkv_come)],
-        [(BF, [lambda p, j=j: (0, p[2] ^ j, 0, rows)]) for j in range(4)],
+        [
+            (BF, [lambda p, j=j, s=s: (0, (p[2] ^ j) * cuts_of + s, 0, step) for s in range(cuts_of)])
+            for j in range(4)
+        ],
         "qkv_join3",
-        sums=(own_sums, 4),
+        sums=(own_sums, 4 * cuts_of),
         after=(merge_last,),
     )
     cuts = [cuts[0]] + [swap(cuts[j], "wide", 2 * j) for j in (1, 2, 3)]

time: 229 us -> 229 us (level)
  starting transfers between devices: 45.3 us -> 50.5 us
  waiting for transfers between devices: 76 us -> 71.9 us
    ppermute x36, starting transfers between devices: 32 us -> 37.2 us  [swap(): return lax.ppermute(array, axis, [(i, i ^ mask) for i in range(size)])]
    ppermute x36, waiting for transfers between devices: 49.6 us -> 45.7 us  [swap(): return lax.ppermute(array, axis, [(i, i ^ mask) for i in range(size)])]
    unnamed x130 -> x128, local copies, waits for them, and re-layouts: 17 us -> 15.9 us
  transfers between devices with their start and end apart: 45 -> 45, of which waited for: 17 -> 18; matrix products, arithmetic and copies ran while one was open for 3% -> 3% of each run, Pallas kernels for 28% -> 28%
where the time goes in v1:
time: 229 us
  Pallas kernels  82.4 us (36%)
  waiting for transfers between devices  71.9 us (31%)
  starting transfers between devices  50.5 us (22%)
  local copies, waits for them, and re-layouts  18 us (8%)
  other arithmetic  4.35 us (2%)
    pallas_call x37, Pallas kernels, whole(): pl.pallas_call(body, in_specs=[pl.BlockSpec(memory_space=pltpu.SMEM)] + [...  82.4 us
    ppermute x36, waiting for transfers between devices, swap(): return lax.ppermute(array, axis, [(i, i ^ mask) for i in range(size)])  45.7 us
    ppermute x36, starting transfers between devices, swap(): return lax.ppermute(array, axis, [(i, i ^ mask) for i in range(size)])  37.2 us
    ppermute x9, waiting for transfers between devices, turn(): lax.ppermute(array, axis, [(i, (i + step) % size) for i in range(size)])  26.1 us
    unnamed x128, local copies, waits for them, and re-layouts  15.9 us
    ppermute x9, starting transfers between devices, turn(): lax.ppermute(array, axis, [(i, (i + step) % size) for i in range(size)])  13.3 us
  transfers between devices with their start and end apart: 45, of which 18 were waited for; matrix products, arithmetic and copies ran while one was open for 3% of the time, Pallas kernels for 28%

profile of v1, /device:TPU:0, one launch (start us, length us, event | category | flops | bytes accessed | tf_op | source)
XLA Modules:
  0.0 228.7 jit_solution(18015774559277100467)
XLA Ops:
  3.3 5.1 %collective-permute-start.2 = (bf16[48,1024]{1,0:T(8,128)(2,1)S(1)}, bf16[48,1024]{1,0:T(8,128)(2,1)S(1)}, u32[]{:S(2)}, u32[]{:S(2)}) collective-permute-start(bf16[48,1024]{1,0:T(8,128)(2,1)S(1)} %pack.1.refs_0_), channel_id=1, source_target_pairs={{0,3},{1,0},{2,1},{3,2},{4,7},{5,4},{6,5},{7,6},{8,11},{9,8},{10,9... | collective-permute-start | bytes 294920 | tf_op jit(solution)/shard_map/ppermute | solution.py:127
  9.8 3.0 %copy-done.10 = bf16[1024,3072]{1,0:T(8,128)(2,1)S(1)} copy-done((bf16[1024,3072]{1,0:T(8,128)(2,1)S(1)}, bf16[1024,3072]{1,0:T(8,128)(2,1)}, u32[]{:S(2)}) %copy-start.10) | copy-done | bytes 6291480
  15.0 4.7 %front.1 = (bf16[200,2048]{1,0:T(8,128)(2,1)S(1)}, f32[200,1024]{1,0:T(8,128)S(1)}, bf16[200,1024]{1,0:T(8,128)(2,1)S(1)}, bf16[200,3072]{1,0:T(8,128)(2,1)S(1)}) custom-call(s32[3]{0:T(128)S(1)} %pad_add_fusion.place_ref, bf16[200,2048]{1,0:T(8,128)(2,1)S(1)} %bitcast.39, f32[1,2048]{1,0:T(1,128)S(1)} %bitcast.47, f32[1,2048]{1,0:T(1,128)S(1)} %bitcast.46, ...), custom_call_target="tpu_custom_call" | custom-call | flops 99999997952 | tf_op jit(solution)/shard_map/front/pallas_call | solution.py:88
  26.2 5.9 %attend.1 = (bf16[200,1024]{1,0:T(8,128)(2,1)S(1)}, f32[52,2,8,112,128]{4,3,2,1,0:T(8,128)}) custom-call(s32[3]{0:T(128)S(1)} %pad_add_fusion.place_ref, bf16[200,3072]{1,0:T(8,128)(2,1)S(1)} %get-tuple-element.118.refs_0_, f32[3584,128]{1,0:T(8,128)S(1)} %spread.1.refs_1_, f32[2,1,128]{2,1,0:T(1,128)S(1)} %and_select_fusion.refs_2_), custom_call_target="tpu_custom_call" | custom-call | flops 99999997952 | tf_op jit(solution)/shard_map/attend/pallas_call | solution.py:88
  40.7 2.8 %collective-permute-start.9 = (bf16[200,1024]{1,0:T(8,128)(2,1)S(1)}, bf16[200,1024]{1,0:T(8,128)(2,1)S(1)}, u32[]{:S(2)}, u32[]{:S(2)}) collective-permute-start(bf16[200,1024]{1,0:T(8,128)(2,1)S(1)} %get-tuple-element.126.refs_2_.refs_0_), channel_id=1, source_target_pairs={{0,3},{1,0},{2,1},{3,2},{4,7},{5,4},{6,5},{7,6},{8,11},{9,8},{10,9... | collective-permute-start | bytes 1228808 | tf_op jit(solution)/shard_map/ppermute | solution.py:127
  44.7 4.7 %collective-permute-done.12.refs_2_ = bf16[2,200,512]{2,1,0:T(8,128)(2,1)S(1)} collective-permute-done((bf16[2,200,512]{2,1,0:T(8,128)(2,1)S(1)}, bf16[2,200,512]{2,1,0:T(8,128)(2,1)S(1)}, u32[]{:S(2)}, u32[]{:S(2)}) %collective-permute-start.12) | collective-permute-done | bytes 409632 | tf_op jit(solution)/shard_map/ppermute | solution.py:122
  53.3 3.5 %slope.1 = (bf16[832,1024]{1,0:T(8,128)(2,1)S(1)}, bf16[200,1024]{1,0:T(8,128)(2,1)S(1)}, f32[832,1024]{1,0:T(8,128)S(1)}) custom-call(s32[3]{0:T(128)S(1)} %pad_add_fusion.place_ref, bf16[800,1024]{1,0:T(8,128)(2,1)S(1)} %copy-done.15, bf16[1024,1024]{1,0:T(8,128)(2,1)S(1)} %copy-done.14, bf16[200,1024]{1,0:T(8,128)(2,1)S(1)} %get-tuple-element.126.refs_2_.refs_0_), custom_call_target="tpu_custom_call" | custom-call | flops 99999997952 | tf_op jit(solution)/shard_map/slope/pallas_call | solution.py:88
  56.9 23.0 %collective-permute-done.8.refs_2_ = bf16[200,1024]{1,0:T(8,128)(2,1)S(1)} collective-permute-done((bf16[200,1024]{1,0:T(8,128)(2,1)S(1)}, bf16[200,1024]{1,0:T(8,128)(2,1)S(1)}, u32[]{:S(2)}, u32[]{:S(2)}) %collective-permute-start.8) | collective-permute-done | bytes 409632 | tf_op jit(solution)/shard_map/ppermute | solution.py:127
  79.9 8.0 %feed.1 = (bf16[832,1024]{1,0:T(8,128)(2,1)S(1)}, bf16[832,1024]{1,0:T(8,128)(2,1)S(1)}, bf16[832,1024]{1,0:T(8,128)(2,1)S(1)}, f32[1,1024]{1,0:T(1,128)S(1)}, b...) custom-call(s32[3]{0:T(128)S(1)} %pad_add_fusion.place_ref, ...), custom_call_target="tpu_custom_call" | custom-call | flops 99999997952 | tf_op jit(solution)/shard_map/feed/pallas_call | solution.py:88
  91.3 2.5 %second.1 = (bf16[2,200,1024]{2,1,0:T(8,128)(2,1)S(1)}, bf16[2,200,1024]{2,1,0:T(8,128)(2,1)S(1)}) custom-call(s32[3]{0:T(128)S(1)} %pad_add_fusion.place_ref, bf16[832,1024]{1,0:T(8,128)(2,1)S(1)} %get-tuple-element.131.refs_0_, bf16[1024,1024]{1,0:T(8,128)(2,1)S(1)} %copy-done.14), custom_call_target="tpu_custom_call" | custom-call | flops 99999997952 | tf_op jit(solution)/shard_map/second/pallas_call | solution.py:88
  93.7 3.8 %fc2_grad.1 = (f32[4,128,1024]{2,1,0:T(8,128)S(1)}, bf16[4,128,1024]{2,1,0:T(8,128)(2,1)S(1)}) custom-call(s32[3]{0:T(128)S(1)} %pad_add_fusion.place_ref, bf16[832,1024]{1,0:T(8,128)(2,1)S(1)} %get-tuple-element.131.refs_0_, bf16[832,1024]{1,0:T(8,128)(2,1)S(1)} %get-tuple-element.145.refs_1_), custom_call_target="tpu_custom_call" | custom-call | flops 99999997952 | tf_op jit(solution)/shard_map/fc2_grad/pallas_call | solution.py:88
  97.7 3.8 %fc1_grad.1 = (f32[4,128,1024]{2,1,0:T(8,128)S(1)}, bf16[4,128,1024]{2,1,0:T(8,128)(2,1)S(1)}) custom-call(s32[3]{0:T(128)S(1)} %pad_add_fusion.place_ref, bf16[832,1024]{1,0:T(8,128)(2,1)S(1)} %get-tuple-element.138.refs_0_, bf16[832,1024]{1,0:T(8,128)(2,1)S(1)} %get-tuple-element.139.refs_1_), custom_call_target="tpu_custom_call" | custom-call | flops 99999997952 | tf_op jit(solution)/shard_map/fc1_grad/pallas_call | solution.py:88
  106.0 10.7 %collective-permute-done.20.refs_1_ = bf16[2,128,1024]{2,1,0:T(8,128)(2,1)S(1)} collective-permute-done((bf16[2,128,1024]{2,1,0:T(8,128)(2,1)S(1)}, bf16[2,128,1024]{2,1,0:T(8,128)(2,1)S(1)}, u32[]{:S(2)}, u32[]{:S(2)}) %collective-permute-start.20) | collective-permute-done | bytes 524320 | tf_op jit(solution)/shard_map/ppermute | solution.py:122
  121.7 3.1 %collective-permute-done.15.refs_2_ = bf16[200,1024]{1,0:T(8,128)(2,1)} collective-permute-done((bf16[200,1024]{1,0:T(8,128)(2,1)}, bf16[200,1024]{1,0:T(8,128)(2,1)}, u32[]{:S(2)}, u32[]{:S(2)}) %collective-permute-start.15) | collective-permute-done | bytes 409632 | tf_op jit(solution)/shard_map/ppermute | solution.py:127
  124.9 3.1 %back2.1 = (f32[208,1024]{1,0:T(8,128)S(1)}, bf16[200,1024]{1,0:T(8,128)(2,1)S(1)}, bf16[2,200,1024]{2,1,0:T(8,128)(2,1)S(1)}) custom-call(s32[3]{0:T(128)S(1)} %pad_add_fusion.place_ref, bf16[200,1024]{1,0:T(8,128)(2,1)S(1)} %get-tuple-element.133.refs_0_, bf16[200,1024]{1,0:T(8,128)(2,1)} %collective-permute-done.14.refs_1_, ...), custom_call_target="tpu_custom_call", output_to_operand_aliasing={{2}: (13, {})} | custom-call | flops 5000000000 | tf_op jit(solution)/shard_map/back2/pallas_call | solution.py:88
  128.7 9.6 %attend_back.1 = (bf16[200,768]{1,0:T(8,128)(2,1)S(1)}, bf16[200,768]{1,0:T(8,128)(2,1)S(1)}, bf16[200,768]{1,0:T(8,128)(2,1)S(1)}, bf16[200,768]{1,0:T(8,128)(2,1)S(1)}, f32[32,384]{1,0:T(8,128)S(1)}) custom-call(s32[3]{0:T(128)S(1)} %pad_add_fusion.place_ref, bf16[200,3072]{1,0:T(8,128)(2,1)S(1)} %get-tuple-element.118.refs_0_, ...), custom_call_target="tpu_custom_call" | custom-call | flops 5000000000 | tf_op jit(solution)/shard_map/attend_back/pallas_call | solution.py:88
  141.9 4.2 %back1.1 = (bf16[200,1024]{1,0:T(8,128)(2,1)S(1)}, f32[5,1024]{1,0:T(8,128)S(1)}) custom-call(s32[3]{0:T(128)S(1)} %pad_add_fusion.place_ref, bf16[200,768]{1,0:T(8,128)(2,1)S(1)} %get-tuple-element.158.refs_0_.refs_4_, bf16[200,768]{1,0:T(8,128)(2,1)S(1)} %get-tuple-element.159.refs_1_, bf16[200,768]{1,0:T(8,128)(2,1)S(1)} %get-tuple-element.160.refs_2_, ...), custom_call_target="tpu_custom_call" | custom-call | flops 20000000000 | tf_op jit(solution)/shard_map/back1/pallas_call | solution.py:88
  146.1 3.4 %back0.1 = (bf16[200,2048]{1,0:T(8,128)(2,1)S(1)}, f32[4,1024]{1,0:T(4,128)S(1)}) custom-call(s32[3]{0:T(128)S(1)} %pad_add_fusion.place_ref, bf16[200,1024]{1,0:T(8,128)(2,1)S(1)} %get-tuple-element.163.refs_0_.refs_2_.refs_10_, bf16[200,2048]{1,0:T(8,128)(2,1)S(1)} %bitcast.40, f32[1,2048]{1,0:T(1,128)S(1)} %bitcast.48, bf16[2048,1024]{1,0:T(8,128)(2,1)S(1)} %copy-done.12), custom_call_target="tpu_custom_call" | custom-call | flops 20000000000 | tf_op jit(solution)/shard_map/back0/pallas_call | solution.py:88
  156.8 4.4 %qkv_grad.1 = (f32[4,128,768]{2,1,0:T(8,128)S(1)}, bf16[5,128,768]{2,1,0:T(8,128)(2,1)}) custom-call(s32[3]{0:T(128)S(1)} %pad_add_fusion.place_ref, bf16[200,1024]{1,0:T(8,128)(2,1)S(1)} %get-tuple-element.128.refs_0_, bf16[2,200,1024]{2,1,0:T(8,128)(2,1)S(1)} %copy-done.5, bf16[2,200,1024]{2,1,0:T(8,128)(2,1)S(1)} %collective-permute-done.11.refs_7_.refs_2_.refs_3_, ...), custom_call_target="tpu_custom_call" | custom-call | flops 5000000000 | tf_op jit(solution)/shard_map/qkv_grad/pallas_call | solution.py:88
  172.4 5.4 %collective-permute-done.31.refs_7_ = bf16[200,1024]{1,0:T(8,128)(2,1)S(1)} collective-permute-done((bf16[200,1024]{1,0:T(8,128)(2,1)}, bf16[200,1024]{1,0:T(8,128)(2,1)S(1)}, u32[]{:S(2)}, u32[]{:S(2)}) %collective-permute-start.31) | collective-permute-done | bytes 409632 | tf_op jit(solution)/shard_map/ppermute | solution.py:122
  177.7 7.3 %collective-permute-done.30.refs_6_ = bf16[200,1024]{1,0:T(8,128)(2,1)S(1)} collective-permute-done((bf16[200,1024]{1,0:T(8,128)(2,1)}, bf16[200,1024]{1,0:T(8,128)(2,1)S(1)}, u32[]{:S(2)}, u32[]{:S(2)}) %collective-permute-start.30) | collective-permute-done | bytes 409632 | tf_op jit(solution)/shard_map/ppermute | solution.py:122
  195.8 2.5 %collective-permute-start.36 = (bf16[2,64,1024]{2,1,0:T(8,128)(2,1)}, bf16[2,64,1024]{2,1,0:T(8,128)(2,1)}, u32[]{:S(2)}, u32[]{:S(2)}) collective-permute-start(bf16[2,64,1024]{2,1,0:T(8,128)(2,1)} %get-tuple-element.186.refs_2_), channel_id=1, source_target_pairs={{0,1},{1,0},{2,3},{3,2},{4,5},{5,4},{6,7},{7,6},{8,9},{9,8},{10,11... | collective-permute-start | bytes 786440 | tf_op jit(solution)/shard_map/ppermute | solution.py:122
  198.2 4.2 %collective-permute-done.41.refs_1_ = bf16[8,32,1024]{2,1,0:T(8,128)(2,1)S(1)} collective-permute-done((bf16[8,32,1024]{2,1,0:T(8,128)(2,1)S(1)}, bf16[8,32,1024]{2,1,0:T(8,128)(2,1)S(1)}, u32[]{:S(2)}, u32[]{:S(2)}) %collective-permute-start.41) | collective-permute-done | bytes 524320 | tf_op jit(solution)/shard_map/ppermute | solution.py:122
  222.8 2.5 %collective-permute-start.44 = (bf16[1,32,1024]{2,1,0:T(8,128)(2,1)S(1)}, bf16[1,32,1024]{2,1,0:T(8,128)(2,1)S(1)}, u32[]{:S(2)}, u32[]{:S(2)}) collective-permute-start(bf16[1,32,1024]{2,1,0:T(8,128)(2,1)S(1)} %get-tuple-element.208), channel_id=1, source_target_pairs={{0,2},{1,3},{2,0},{3,1},{4,6},{5,7},{6,4},{7,5},{8,10},{9,11},{10,... | collective-permute-start | bytes 196616 | tf_op jit(solution)/shard_map/ppermute | solution.py:122
  (248 shorter events, 95.8 us)
Async XLA Ops:
  3.3 16.5 %collective-permute-start.2 = (bf16[48,1024]{1,0:T(8,128)(2,1)S(1)}, bf16[48,1024]{1,0:T(8,128)(2,1)S(1)}, u32[]{:S(2)}, u32[]{:S(2)}) collective-permute-start(bf16[48,1024]{1,0:T(8,128)(2,1)S(1)} %pack.1.refs_0_), channel_id=1, source_target_pairs={{0,3},{1,0},{2,1},{3,2},{4,7},{5,4},{6,5},{7,6},{8,11},{9,8},{10,9... | collective-permute-start | bytes 294920 | tf_op jit(solution)/shard_map/ppermute | solution.py:127
  40.7 16.1 %collective-permute-start.9 = (bf16[200,1024]{1,0:T(8,128)(2,1)S(1)}, bf16[200,1024]{1,0:T(8,128)(2,1)S(1)}, u32[]{:S(2)}, u32[]{:S(2)}) collective-permute-start(bf16[200,1024]{1,0:T(8,128)(2,1)S(1)} %get-tuple-element.126.refs_2_.refs_0_), channel_id=1, source_target_pairs={{0,3},{1,0},{2,1},{3,2},{4,7},{5,4},{6,5},{7,6},{8,11},{9,8},{10,9... | collective-permute-start | bytes 1228808 | tf_op jit(solution)/shard_map/ppermute | solution.py:127
  43.5 36.4 %collective-permute-start.8 = (bf16[200,1024]{1,0:T(8,128)(2,1)S(1)}, bf16[200,1024]{1,0:T(8,128)(2,1)S(1)}, u32[]{:S(2)}, u32[]{:S(2)}) collective-permute-start(bf16[200,1024]{1,0:T(8,128)(2,1)S(1)} %get-tuple-element.126.refs_2_.refs_0_), channel_id=1, source_target_pairs={{0,2},{1,3},{2,0},{3,1},{4,6},{5,7},{6,4},{7,5},{8,10},{9,11},{10,... | collective-permute-start | bytes 1228808 | tf_op jit(solution)/shard_map/ppermute | solution.py:127
  44.7 35.3 %collective-permute-start.7 = (bf16[200,1024]{1,0:T(8,128)(2,1)S(1)}, bf16[200,1024]{1,0:T(8,128)(2,1)S(1)}, u32[]{:S(2)}, u32[]{:S(2)}) collective-permute-start(bf16[200,1024]{1,0:T(8,128)(2,1)S(1)} %get-tuple-element.126.refs_2_.refs_0_), channel_id=1, source_target_pairs={{0,1},{1,2},{2,3},{3,0},{4,5},{5,6},{6,7},{7,4},{8,9},{9,10},{10,1... | collective-permute-start | bytes 1228808 | tf_op jit(solution)/shard_map/ppermute | solution.py:127
  50.2 29.7 %collective-permute-start.13 = (bf16[2,200,512]{2,1,0:T(8,128)(2,1)S(1)}, bf16[2,200,512]{2,1,0:T(8,128)(2,1)S(1)}, u32[]{:S(2)}, u32[]{:S(2)}) collective-permute-start(bf16[2,200,512]{2,1,0:T(8,128)(2,1)S(1)} %pad_maximum_fusion.1), channel_id=1, source_target_pairs={{0,8},{4,12},{8,0},{12,4},{16,24},{20,28},{24,16},{28,20},{1,9},{5... | collective-permute-start | bytes 1228808 | tf_op jit(solution)/shard_map/ppermute | solution.py:122
  51.9 28.0 %collective-permute-start.11 = (bf16[2,200,1024]{2,1,0:T(8,128)(2,1)S(1)}, bf16[2,200,1024]{2,1,0:T(8,128)(2,1)S(1)}, u32[]{:S(2)}, u32[]{:S(2)}) collective-permute-start(bf16[2,200,1024]{2,1,0:T(8,128)(2,1)S(1)} %pad_maximum_fusion.refs_1_), channel_id=1, source_target_pairs={{0,16},{4,20},{8,24},{12,28},{16,0},{20,4},{24,8},{28,12},{1,17},{... | collective-permute-start | bytes 2457608 | tf_op jit(solution)/shard_map/ppermute | solution.py:122
  88.0 33.7 %collective-permute-start.14 = (bf16[200,1024]{1,0:T(8,128)(2,1)}, bf16[200,1024]{1,0:T(8,128)(2,1)}, u32[]{:S(2)}, u32[]{:S(2)}) collective-permute-start(bf16[200,1024]{1,0:T(8,128)(2,1)} %get-tuple-element.134), channel_id=1, source_target_pairs={{0,3},{1,0},{2,1},{3,2},{4,7},{5,4},{6,5},{7,6},{8,11},{9,8},{10,9... | collective-permute-start | bytes 1228808 | tf_op jit(solution)/shard_map/ppermute | solution.py:127
  88.0 36.8 %collective-permute-start.15 = (bf16[200,1024]{1,0:T(8,128)(2,1)}, bf16[200,1024]{1,0:T(8,128)(2,1)}, u32[]{:S(2)}, u32[]{:S(2)}) collective-permute-start(bf16[200,1024]{1,0:T(8,128)(2,1)} %get-tuple-element.135), channel_id=1, source_target_pairs={{0,2},{1,3},{2,0},{3,1},{4,6},{5,7},{6,4},{7,5},{8,10},{9,11},{10,... | collective-permute-start | bytes 1228808 | tf_op jit(solution)/shard_map/ppermute | solution.py:127
  89.2 35.6 %collective-permute-start.16 = (bf16[200,1024]{1,0:T(8,128)(2,1)}, bf16[200,1024]{1,0:T(8,128)(2,1)}, u32[]{:S(2)}, u32[]{:S(2)}) collective-permute-start(bf16[200,1024]{1,0:T(8,128)(2,1)} %get-tuple-element.136), channel_id=1, source_target_pairs={{0,1},{1,2},{2,3},{3,0},{4,5},{5,6},{6,7},{7,4},{8,9},{9,10},{10,1... | collective-permute-start | bytes 1228808 | tf_op jit(solution)/shard_map/ppermute | solution.py:127
  102.8 13.9 %collective-permute-start.20 = (bf16[2,128,1024]{2,1,0:T(8,128)(2,1)S(1)}, bf16[2,128,1024]{2,1,0:T(8,128)(2,1)S(1)}, u32[]{:S(2)}, u32[]{:S(2)}) collective-permute-start(bf16[2,128,1024]{2,1,0:T(8,128)(2,1)S(1)} %get-tuple-element.149), channel_id=1, source_target_pairs={{0,16},{4,20},{8,24},{12,28},{16,0},{20,4},{24,8},{28,12},{1,17},{... | collective-permute-start | bytes 1572872 | tf_op jit(solution)/shard_map/ppermute | solution.py:122
  105.1 14.3 %collective-permute-start.18 = (bf16[2,128,1024]{2,1,0:T(8,128)(2,1)S(1)}, bf16[2,128,1024]{2,1,0:T(8,128)(2,1)S(1)}, u32[]{:S(2)}, u32[]{:S(2)}) collective-permute-start(bf16[2,128,1024]{2,1,0:T(8,128)(2,1)S(1)} %get-tuple-element.143), channel_id=1, source_target_pairs={{0,8},{4,12},{8,0},{12,4},{16,24},{20,28},{24,16},{28,20},{1,9},{5... | collective-permute-start | bytes 1572872 | tf_op jit(solution)/shard_map/ppermute | solution.py:122
  127.9 23.8 %collective-permute-start.21 = (bf16[2,200,1024]{2,1,0:T(8,128)(2,1)S(1)}, bf16[2,200,1024]{2,1,0:T(8,128)(2,1)S(1)}, u32[]{:S(2)}, u32[]{:S(2)}) collective-permute-start(bf16[2,200,1024]{2,1,0:T(8,128)(2,1)S(1)} %get-tuple-element.152), channel_id=1, source_target_pairs={{0,1},{1,0},{2,3},{3,2},{4,5},{5,4},{6,7},{7,6},{8,9},{9,8},{10,11... | collective-permute-start | bytes 2457608 | tf_op jit(solution)/shard_map/ppermute | solution.py:122
  138.3 16.8 %collective-permute-start.25 = (bf16[200,768]{1,0:T(8,128)(2,1)S(1)}, bf16[200,768]{1,0:T(8,128)(2,1)S(1)}, u32[]{:S(2)}, u32[]{:S(2)}) collective-permute-start(bf16[200,768]{1,0:T(8,128)(2,1)S(1)} %get-tuple-element.159.refs_1_), channel_id=1, source_target_pairs={{0,8},{4,12},{8,0},{12,4},{16,24},{20,28},{24,16},{28,20},{1,9},{5... | collective-permute-start | bytes 921608 | tf_op jit(solution)/shard_map/ppermute | solution.py:122
  139.2 15.9 %collective-permute-start.26 = (bf16[200,768]{1,0:T(8,128)(2,1)S(1)}, bf16[200,768]{1,0:T(8,128)(2,1)S(1)}, u32[]{:S(2)}, u32[]{:S(2)}) collective-permute-start(bf16[200,768]{1,0:T(8,128)(2,1)S(1)} %get-tuple-element.160.refs_2_), channel_id=1, source_target_pairs={{0,16},{4,20},{8,24},{12,28},{16,0},{20,4},{24,8},{28,12},{1,17},{... | collective-permute-start | bytes 921608 | tf_op jit(solution)/shard_map/ppermute | solution.py:122
  139.8 15.3 %collective-permute-start.27 = (bf16[200,768]{1,0:T(8,128)(2,1)S(1)}, bf16[200,768]{1,0:T(8,128)(2,1)S(1)}, u32[]{:S(2)}, u32[]{:S(2)}) collective-permute-start(bf16[200,768]{1,0:T(8,128)(2,1)S(1)} %get-tuple-element.161.refs_3_), channel_id=1, source_target_pairs={{0,24},{4,28},{8,16},{12,20},{16,8},{20,12},{24,0},{28,4},{1,25},{... | collective-permute-start | bytes 921608 | tf_op jit(solution)/shard_map/ppermute | solution.py:122
  162.5 24.6 %collective-permute-start.22 = (bf16[1,200,1024]{2,1,0:T(8,128)(2,1)}, bf16[1,200,1024]{2,1,0:T(8,128)(2,1)S(1)}, u32[]{:S(2)}, u32[]{:S(2)}) collective-permute-start(bf16[1,200,1024]{2,1,0:T(8,128)(2,1)} %copy-done.27), channel_id=1, source_target_pairs={{0,2},{1,3},{2,0},{3,1},{4,6},{5,7},{6,4},{7,5},{8,10},{9,11},{10,... | collective-permute-start | bytes 1228808 | tf_op jit(solution)/shard_map/ppermute | solution.py:122
  164.2 13.5 %collective-permute-start.31 = (bf16[200,1024]{1,0:T(8,128)(2,1)}, bf16[200,1024]{1,0:T(8,128)(2,1)S(1)}, u32[]{:S(2)}, u32[]{:S(2)}) collective-permute-start(bf16[200,1024]{1,0:T(8,128)(2,1)} %copy-done.28), channel_id=1, source_target_pairs={{0,24},{4,28},{8,16},{12,20},{16,8},{20,12},{24,0},{28,4},{1,25},{... | collective-permute-start | bytes 1228808 | tf_op jit(solution)/shard_map/ppermute | solution.py:122
  164.9 20.2 %collective-permute-start.30 = (bf16[200,1024]{1,0:T(8,128)(2,1)}, bf16[200,1024]{1,0:T(8,128)(2,1)S(1)}, u32[]{:S(2)}, u32[]{:S(2)}) collective-permute-start(bf16[200,1024]{1,0:T(8,128)(2,1)} %copy-done.28), channel_id=1, source_target_pairs={{0,16},{4,20},{8,24},{12,28},{16,0},{20,4},{24,8},{28,12},{1,17},{... | collective-permute-start | bytes 1228808 | tf_op jit(solution)/shard_map/ppermute | solution.py:122
  166.3 18.7 %collective-permute-start.29 = (bf16[200,1024]{1,0:T(8,128)(2,1)}, bf16[200,1024]{1,0:T(8,128)(2,1)S(1)}, u32[]{:S(2)}, u32[]{:S(2)}) collective-permute-start(bf16[200,1024]{1,0:T(8,128)(2,1)} %copy-done.28), channel_id=1, source_target_pairs={{0,8},{4,12},{8,0},{12,4},{16,24},{20,28},{24,16},{28,20},{1,9},{5... | collective-permute-start | bytes 1228808 | tf_op jit(solution)/shard_map/ppermute | solution.py:122
  171.6 19.8 %collective-permute-start.34 = (bf16[19,16,768]{2,1,0:T(8,128)(2,1)S(1)}, bf16[19,16,768]{2,1,0:T(8,128)(2,1)S(1)}, u32[]{:S(2)}, u32[]{:S(2)}) collective-permute-start(bf16[19,16,768]{2,1,0:T(8,128)(2,1)S(1)} %get-tuple-element.175.refs_8_), channel_id=1, source_target_pairs={{0,1},{1,0},{2,3},{3,2},{4,5},{5,4},{6,7},{7,6},{8,9},{9,8},{10,11... | collective-permute-start | bytes 1400840 | tf_op jit(solution)/shard_map/ppermute | solution.py:122
  188.1 14.3 %collective-permute-start.41 = (bf16[8,32,1024]{2,1,0:T(8,128)(2,1)S(1)}, bf16[8,32,1024]{2,1,0:T(8,128)(2,1)S(1)}, u32[]{:S(2)}, u32[]{:S(2)}) collective-permute-start(bf16[8,32,1024]{2,1,0:T(8,128)(2,1)S(1)} %copy-done.24), channel_id=1, source_target_pairs={{0,8},{4,12},{8,0},{12,4},{16,24},{20,28},{24,16},{28,20},{1,9},{5... | collective-permute-start | bytes 1572872 | tf_op jit(solution)/shard_map/ppermute | solution.py:122
  193.4 16.9 %collective-permute-start.35 = (bf16[11,16,768]{2,1,0:T(8,128)(2,1)S(1)}, bf16[11,16,768]{2,1,0:T(8,128)(2,1)S(1)}, u32[]{:S(2)}, u32[]{:S(2)}) collective-permute-start(bf16[11,16,768]{2,1,0:T(8,128)(2,1)S(1)} %get-tuple-element.180.refs_2_), channel_id=1, source_target_pairs={{0,2},{1,3},{2,0},{3,1},{4,6},{5,7},{6,4},{7,5},{8,10},{9,11},{10,... | collective-permute-start | bytes 811016 | tf_op jit(solution)/shard_map/ppermute | solution.py:122
  195.8 13.3 %collective-permute-start.36 = (bf16[2,64,1024]{2,1,0:T(8,128)(2,1)}, bf16[2,64,1024]{2,1,0:T(8,128)(2,1)}, u32[]{:S(2)}, u32[]{:S(2)}) collective-permute-start(bf16[2,64,1024]{2,1,0:T(8,128)(2,1)} %get-tuple-element.186.refs_2_), channel_id=1, source_target_pairs={{0,1},{1,0},{2,3},{3,2},{4,5},{5,4},{6,7},{7,6},{8,9},{9,8},{10,11... | collective-permute-start | bytes 786440 | tf_op jit(solution)/shard_map/ppermute | solution.py:122
  210.2 15.1 %collective-permute-start.40 = (bf16[1,64,1024]{2,1,0:T(8,128)(2,1)S(1)}, bf16[1,64,1024]{2,1,0:T(8,128)(2,1)S(1)}, u32[]{:S(2)}, u32[]{:S(2)}) collective-permute-start(bf16[1,64,1024]{2,1,0:T(8,128)(2,1)S(1)} %get-tuple-element.187.refs_3_.refs_2_), channel_id=1, source_target_pairs={{0,2},{1,3},{2,0},{3,1},{4,6},{5,7},{6,4},{7,5},{8,10},{9,11},{10,... | collective-permute-start | bytes 393224 | tf_op jit(solution)/shard_map/ppermute | solution.py:122
  (84 other events, 544.3 us)
